TPU v7x, 32 devices: a whole 2x2x4 slice. The times are simulated.
32 devices in a mesh: groups: 2 (over y), tile: 4 (over z), chan: 2 (over x), sub: 2 (over core).
Axes of the slice: x: 2, y: 2, z: 4, core: 2. Of those that a mesh axis runs over, the one named last changes fastest.
Arguments:
- activations: bfloat16 [256, 32, 256], P('chan', ('groups', 'tile'), 'sub'), parts along dimension 1, may hold values from -6 to 6
- out_grad: bfloat16 [256, 32, 256], P('chan', ('groups', 'tile'), 'sub'), parts along dimension 1, may hold values from -6 to 6
- weight: bfloat16 [256, 6912], P('chan'), may hold values from -0.078125 to 0.078125
Outputs:
- conv_out: bfloat16 [256, 32, 256], P('chan', ('groups', 'tile'), 'sub'), parts along dimension 1
- input_grad: bfloat16 [256, 32, 256], P('chan', ('groups', 'tile'), 'sub'), parts along dimension 1
- weight_grad: float32 [512, 6912], P(('groups', 'chan')), parts along dimension 0
There are 2 independent parts, one for each index of `groups`. A program takes and returns all parts, laid end to end along the dimension named above; an argument that names none is the same for every part. Nothing has to cross between parts.
All inputs are finite; a program needn't handle non-finite values.
Results may differ from a plain program's by a relative error of at most 0.0034.
Values may be sent and summed in bfloat16 or wider, within the bound.
No kernel may reach another device: no remote copies, remote signals or barrier semaphores. Data moves between devices by JAX's collectives and lax.ppermute only.
A program may use at most 64 MiB of HBM per device.

v0:
```python
import math

import jax
import jax.numpy as jnp
from jax import lax
from jax.sharding import PartitionSpec as P

ZS = 4


def with_halo(cells, sides, width):
    for axis, dim in sides:
        count = lax.axis_size(axis)
        ends = count - 1
        head = lax.slice_in_dim(cells, 0, width, axis=dim)
        tail = lax.slice_in_dim(cells, cells.shape[dim] - width, cells.shape[dim], axis=dim)
        cells = jnp.concatenate(
            [
                lax.ppermute(tail, axis, [(i, (i + 1) % count) for i in range(ends)]),
                cells,
                lax.ppermute(head, axis, [((i + 1) % count, i) for i in range(ends)]),
            ],
            axis=dim,
        )
    return cells


def extend(field):
    wider = with_halo(field, (("sub", 2),), ZS)
    return with_halo(wider, (("tile", 1),), 1)


def flat_pad(padded):
    return jnp.pad(padded, ((0, 0), (0, 0), (1, 1)))


def tap_window(flatten, tap_idx, direction, x_planes, span_yz):
    plane_idx = tap_idx // 9
    row_idx = tap_idx // 3 % 3
    depth_idx = tap_idx % 3
    shift_x = direction * (plane_idx - 1)
    shift_y = direction * (row_idx - 1)
    shift_z = direction * (depth_idx - 1)
    start_col = 1 + (1 + shift_y) * ZS + shift_z
    window = flatten[:, 1 + shift_x : 1 + shift_x + x_planes, start_col : start_col + span_yz]
    z_index = jnp.arange(span_yz) % ZS
    inside = (z_index + shift_z >= 0) & (z_index + shift_z < ZS)
    masked = jnp.where(inside, window, jnp.zeros((), window.dtype))
    return masked.reshape(flatten.shape[0], x_planes * span_yz)


def body(activations, out_grad, weight):
    local_ch, x_planes, span_yz = activations.shape
    rows_y = span_yz // ZS
    cells = x_planes * span_yz
    total_ch = weight.shape[1] // 27
    scale = 1.0 / math.sqrt(x_planes * lax.axis_size("tile") * rows_y * lax.axis_size("sub") * ZS)
    padded_x = extend(activations)
    padded_g = extend(out_grad)
    grad_flat = out_grad.reshape(local_ch, cells)
    by_tap = weight.reshape(local_ch, total_ch, 27).transpose(2, 0, 1)
    piece = lax.all_gather(padded_x, "chan", axis=0, tiled=True)
    output_acc = jnp.zeros((local_ch, cells), jnp.float32)
    flatten = flat_pad(piece)
    updates = []
    for tap_idx in range(27):
        window = tap_window(flatten, tap_idx, 1, x_planes, span_yz)
        columns = by_tap[tap_idx]
        output_acc = output_acc + jnp.dot(columns, window, preferred_element_type=jnp.float32)
        updates.append(
            lax.dot_general(
                grad_flat, window, (((1,), (1,)), ((), ())), preferred_element_type=jnp.float32
            )
        )
    grad_acc = jnp.stack(updates, axis=0)
    output_acc, grad_acc = (output_acc, grad_acc)
    conv_out = output_acc.reshape(activations.shape).astype(jnp.bfloat16)
    local_grad = grad_acc.transpose(1, 2, 0).reshape(local_ch, total_ch * 27) * scale
    weight_grad = lax.psum(local_grad, ("tile", "sub"))
    transposed = weight.reshape(local_ch, total_ch, 27).transpose(2, 1, 0)
    grad_padded = flat_pad(padded_g)
    running = jnp.zeros((lax.axis_size("chan") * local_ch, cells), jnp.float32)
    for tap_idx in range(27):
        window = tap_window(grad_padded, tap_idx, -1, x_planes, span_yz)
        rows_w = transposed[tap_idx]
        running = running + jnp.dot(rows_w, window, preferred_element_type=jnp.float32)
    summed = lax.psum_scatter(running, "chan", scatter_dimension=0, tiled=True)
    input_grad = summed.reshape(activations.shape).astype(jnp.bfloat16)
    return (conv_out, input_grad, weight_grad)


def solution(mesh):
    placed = (
        P("chan", ("groups", "tile"), "sub"),
        P("chan", ("groups", "tile"), "sub"),
        P("chan", None),
    )
    return jax.shard_map(
        body,
        mesh=mesh,
        in_specs=placed,
        out_specs=(
            P("chan", ("groups", "tile"), "sub"),
            P("chan", ("groups", "tile"), "sub"),
            P(("groups", "chan"), None),
        ),
        check_vma=False,
    )
```

profile of v0, /device:TPU:0, one launch (start us, length us, event | category | flops | bytes accessed | tf_op | source)
XLA Modules:
  0.0 232.6 jit_solution(13947181060673366806)
XLA Ops:
  8.0 1.0 copy.148
  9.7 1.3 collective-permute-start.1
  11.0 3.0 %collective-permute-start = (bf16[128,4,4]{0,2,1:T(4,128)(2,1)}, bf16[128,4,4]{0,2,1:T(4,128)(2,1)S(1)}, u32[]{:S(2)}, u32[]{:S(2)}) collective-permute-start(bf16[128,4,4]{0,2,1:T(4,128)(2,1)} %get-tuple-element.142), channel_id=1, source_target_pairs={{0,1},{2,3},{4,5},{6,7},{8,9},{10,11},{12,13},{14,15},{16,17},{18,... | collective-permute-start | bytes 12296 | tf_op jit(solution)/shard_map/ppermute | solution.py:19
  14.0 1.0 copy.179
  15.7 1.3 collective-permute-start.5
  16.9 3.0 %collective-permute-start.4 = (bf16[128,4,4]{0,2,1:T(4,128)(2,1)}, bf16[128,4,4]{0,2,1:T(4,128)(2,1)S(1)}, u32[]{:S(2)}, u32[]{:S(2)}) collective-permute-start(bf16[128,4,4]{0,2,1:T(4,128)(2,1)} %get-tuple-element.140), channel_id=1, source_target_pairs={{0,1},{2,3},{4,5},{6,7},{8,9},{10,11},{12,13},{14,15},{16,17},{18,... | collective-permute-start | bytes 12296 | tf_op jit(solution)/shard_map/ppermute | solution.py:19
  20.5 3.8 %copy.151 = bf16[128,6912]{0,1:T(8,128)(2,1)} copy(bf16[128,6912]{1,0:T(8,128)(2,1)} %param.5) | data formatting | bytes 3538944 | tf_op args[2]
  24.3 2.5 %reshape.181 = bf16[128,256,27]{0,2,1:T(8,128)(2,1)S(1)} reshape(bf16[128,6912]{0,1:T(8,128)(2,1)} %copy.151) | data formatting | bytes 3538944 | tf_op jit(solution)/shard_map/reshape | solution.py:61
  26.9 3.2 %fusion.151 = (bf16[1,128,256]{1,0,2:T(2,128)(2,1)S(1)}, bf16[1,128,256]{1,0,2:T(2,128)(2,1)S(1)}, bf16[1,128,256]{1,0,2:T(2,128)(2,1)S(1)}, bf16[1,128,256]{1,0...) fusion(bf16[27,128,256]{1,0,2:T(8,128)(2,1)S(1)} %bitcast.636), kind=kLoop, calls=%fused_computation.302 | loop fusion | bytes 2490368 | tf_op jit(solution)/shard_map/slice | solution.py:68
  30.1 1.7 fusion.152
  31.9 1.7 fusion.150
  33.6 3.2 %fusion.149 = (bf16[1,256,128]{2,0,1:T(2,128)(2,1)}, bf16[1,256,128]{2,0,1:T(2,128)(2,1)}, bf16[1,256,128]{2,0,1:T(2,128)(2,1)}, bf16[1,256,128]{2,0,1:T(2,128)(...) fusion(bf16[27,256,128]{2,0,1:T(8,128)(2,1)S(1)} %bitcast.639), kind=kLoop, calls=%fused_computation.300 | loop fusion | bytes 2490368 | tf_op jit(solution)/shard_map/slice | solution.py:85
  36.9 1.6 copy.170
  38.6 1.7 copy.169
  40.2 1.7 copy.152
  41.9 1.7 copy.153
  43.5 1.6 copy.154
  45.2 1.6 copy.155
  46.8 1.6 copy.156
  48.4 1.6 copy.157
  50.1 1.7 copy.158
  51.7 1.6 copy.159
  53.4 1.6 copy.160
  55.0 1.6 copy.161
  56.7 1.6 copy.162
  58.3 1.6 copy.163
  59.9 1.6 copy.164
  61.6 1.7 copy.165
  63.2 1.6 copy.166
  64.9 1.7 copy.167
  66.5 0.7 copy.168
  70.2 0.8 copy.175
  71.7 0.8 copy.177
  73.3 1.3 collective-permute-start.3
  74.6 5.6 %collective-permute-start.2 = (bf16[128,1,136]{0,2,1:T(8,128)(2,1)S(1)}, bf16[128,1,136]{0,2,1:T(8,128)(2,1)S(1)}, u32[]{:S(2)}, u32[]{:S(2)}) collective-permute-start(bf16[128,1,136]{0,2,1:T(8,128)(2,1)S(1)} %get-tuple-element.128), channel_id=1, source_target_pairs={{0,4},{4,8},{8,12},{1,5},{5,9},{9,13},{2,6},{6,10},{10,14},{3,7},{... | collective-permute-start | bytes 104456 | tf_op jit(solution)/shard_map/ppermute | solution.py:19
  80.2 1.3 collective-permute-start.7
  81.5 4.6 %collective-permute-start.6 = (bf16[128,1,136]{0,2,1:T(8,128)(2,1)S(1)}, bf16[128,1,136]{0,2,1:T(8,128)(2,1)S(1)}, u32[]{:S(2)}, u32[]{:S(2)}) collective-permute-start(bf16[128,1,136]{0,2,1:T(8,128)(2,1)S(1)} %get-tuple-element.126), channel_id=1, source_target_pairs={{0,4},{4,8},{8,12},{1,5},{5,9},{9,13},{2,6},{6,10},{10,14},{3,7},{... | collective-permute-start | bytes 104456 | tf_op jit(solution)/shard_map/ppermute | solution.py:19
  86.5 6.7 %all_gather.3 = bf16[256,6,136]{0,2,1:T(8,128)(2,1)S(1)} all-gather(bf16[128,6,136]{0,2,1:T(8,128)(2,1)S(1)} %pad_maximum_fusion), channel_id=1, replica_groups=mesh['groups'=2,'tile'=4,'chan'=2,'sub'=2] {'chan'}, dimensions={0}, use_global_device_ids=true | all-gather | bytes 626688 | tf_op jit(solution)/shard_map/all_gather | solution.py:62
  93.2 1.4 slice_select_fusion.1
  94.5 1.5 slice_select_fusion.21
  96.0 1.2 slice_select_fusion
  104.6 1.0 fusion
  106.0 1.3 fusion.49
  107.2 1.2 fusion.48
  108.5 1.2 fusion.47
  109.7 1.3 fusion.46
  111.0 1.3 fusion.45
  112.3 1.3 fusion.44
  113.5 1.2 fusion.43
  120.8 4.1 %copy.239 = f32[128,256,27]{0,2,1:T(8,128)} copy(f32[128,256,27]{0,1,2:T(8,128)S(1)} %multiply_bitcast_fusion) | data formatting | bytes 7077888 | tf_op jit(solution)/shard_map/mul | solution.py:78
  124.9 4.7 %mul.15 = f32[128,6912]{0,1:T(8,128)} reshape(f32[128,256,27]{0,2,1:T(8,128)} %copy.239) | data formatting | bytes 7077888 | tf_op jit(solution)/shard_map/mul | solution.py:78
  129.6 1.9 convolution_bitcast_fusion.18
  131.4 1.9 convolution_bitcast_fusion.19
  133.3 1.9 fusion.147
  135.3 1.4 convolution_add_fusion.31
  136.7 1.2 convolution_add_fusion.30
  138.0 1.2 convolution_add_fusion.29
  139.2 1.2 convolution_add_fusion.28
  140.4 1.1 convolution_add_fusion.27
  146.3 0.8 copy.240
  147.1 1.0 convert_element_type.18
  148.1 0.8 copy.241
  148.9 71.2 %all-reduce.4.cloned.1.call-done = f32[128,6912]{0,1:T(8,128)} async-done(((f32[128,6912]{0,1:T(8,128)}), f32[128,6912]{0,1:T(8,128)}) %all-reduce.4.cloned.1.call-update) | async-done | bytes 3538960 | tf_op jit(solution)/shard_map/psum | solution.py:79
  220.0 5.2 %copy.242 = f32[128,6912]{1,0:T(8,128)} copy(f32[128,6912]{0,1:T(8,128)} %all-reduce.4.cloned.1.call-done) | data formatting | bytes 7077888
  (241 shorter events, 23.9 us)
Async XLA Ops:
  8.0 139.1 %reduce-scatter.2.cloned.1.call-start = ((), (), s32[]{:S(2)}) async-start(), calls=%async_computation.1 | async-start | bytes 786432 | tf_op jit(solution)/shard_map/reduce_scatter | solution.py:87
  9.7 63.5 %collective-permute-start.1 = (bf16[128,4,4]{0,2,1:T(4,128)(2,1)}, bf16[128,4,4]{0,2,1:T(4,128)(2,1)S(1)}, u32[]{:S(2)}, u32[]{:S(2)}) collective-permute-start(bf16[128,4,4]{0,2,1:T(4,128)(2,1)} %get-tuple-element.143), channel_id=1, source_target_pairs={{1,0},{3,2},{5,4},{7,6},{9,8},{11,10},{13,12},{15,14},{17,16},{19,... | collective-permute-start | bytes 12296 | tf_op jit(solution)/shard_map/ppermute | solution.py:21
  11.0 62.3 %collective-permute-start = (bf16[128,4,4]{0,2,1:T(4,128)(2,1)}, bf16[128,4,4]{0,2,1:T(4,128)(2,1)S(1)}, u32[]{:S(2)}, u32[]{:S(2)}) collective-permute-start(bf16[128,4,4]{0,2,1:T(4,128)(2,1)} %get-tuple-element.142), channel_id=1, source_target_pairs={{0,1},{2,3},{4,5},{6,7},{8,9},{10,11},{12,13},{14,15},{16,17},{18,... | collective-permute-start | bytes 12296 | tf_op jit(solution)/shard_map/ppermute | solution.py:19
  15.7 64.5 %collective-permute-start.5 = (bf16[128,4,4]{0,2,1:T(4,128)(2,1)}, bf16[128,4,4]{0,2,1:T(4,128)(2,1)S(1)}, u32[]{:S(2)}, u32[]{:S(2)}) collective-permute-start(bf16[128,4,4]{0,2,1:T(4,128)(2,1)} %get-tuple-element.141), channel_id=1, source_target_pairs={{1,0},{3,2},{5,4},{7,6},{9,8},{11,10},{13,12},{15,14},{17,16},{19,... | collective-permute-start | bytes 12296 | tf_op jit(solution)/shard_map/ppermute | solution.py:21
  16.9 63.2 %collective-permute-start.4 = (bf16[128,4,4]{0,2,1:T(4,128)(2,1)}, bf16[128,4,4]{0,2,1:T(4,128)(2,1)S(1)}, u32[]{:S(2)}, u32[]{:S(2)}) collective-permute-start(bf16[128,4,4]{0,2,1:T(4,128)(2,1)} %get-tuple-element.140), channel_id=1, source_target_pairs={{0,1},{2,3},{4,5},{6,7},{8,9},{10,11},{12,13},{14,15},{16,17},{18,... | collective-permute-start | bytes 12296 | tf_op jit(solution)/shard_map/ppermute | solution.py:19
  36.9 49.2 %copy-start.66 = (pred[128]{0:T(512)(128)(4,1)S(1)}, pred[128]{0:T(512)(128)(4,1)}, u32[]{:S(2)}) copy-start(pred[128]{0:T(512)(128)(4,1)} %get-tuple-element.151) | copy-start | bytes 388
  36.9 49.2 %copy-start.68 = (pred[128]{0:T(512)(128)(4,1)S(1)}, pred[128]{0:T(512)(128)(4,1)}, u32[]{:S(2)}) copy-start(pred[128]{0:T(512)(128)(4,1)} %get-tuple-element.152) | copy-start | bytes 388
  36.9 49.6 %copy-start.70 = (pred[128]{0:T(512)(128)(4,1)}, pred[128]{0:T(512)(128)(4,1)S(1)}, u32[]{:S(2)}) copy-start(pred[128]{0:T(512)(128)(4,1)S(1)} %compare_and_fusion.1) | copy-start | bytes 388
  73.3 13.1 %collective-permute-start.3 = (bf16[128,1,136]{0,2,1:T(8,128)(2,1)S(1)}, bf16[128,1,136]{0,2,1:T(8,128)(2,1)S(1)}, u32[]{:S(2)}, u32[]{:S(2)}) collective-permute-start(bf16[128,1,136]{0,2,1:T(8,128)(2,1)S(1)} %get-tuple-element.129), channel_id=1, source_target_pairs={{4,0},{8,4},{12,8},{5,1},{9,5},{13,9},{6,2},{10,6},{14,10},{7,3},{... | collective-permute-start | bytes 104456 | tf_op jit(solution)/shard_map/ppermute | solution.py:21
  74.6 11.8 %collective-permute-start.2 = (bf16[128,1,136]{0,2,1:T(8,128)(2,1)S(1)}, bf16[128,1,136]{0,2,1:T(8,128)(2,1)S(1)}, u32[]{:S(2)}, u32[]{:S(2)}) collective-permute-start(bf16[128,1,136]{0,2,1:T(8,128)(2,1)S(1)} %get-tuple-element.128), channel_id=1, source_target_pairs={{0,4},{4,8},{8,12},{1,5},{5,9},{9,13},{2,6},{6,10},{10,14},{3,7},{... | collective-permute-start | bytes 104456 | tf_op jit(solution)/shard_map/ppermute | solution.py:19
  80.2 17.1 %collective-permute-start.7 = (bf16[128,1,136]{0,2,1:T(8,128)(2,1)S(1)}, bf16[128,1,136]{0,2,1:T(8,128)(2,1)S(1)}, u32[]{:S(2)}, u32[]{:S(2)}) collective-permute-start(bf16[128,1,136]{0,2,1:T(8,128)(2,1)S(1)} %get-tuple-element.127), channel_id=1, source_target_pairs={{4,0},{8,4},{12,8},{5,1},{9,5},{13,9},{6,2},{10,6},{14,10},{7,3},{... | collective-permute-start | bytes 104456 | tf_op jit(solution)/shard_map/ppermute | solution.py:21
  81.5 15.8 %collective-permute-start.6 = (bf16[128,1,136]{0,2,1:T(8,128)(2,1)S(1)}, bf16[128,1,136]{0,2,1:T(8,128)(2,1)S(1)}, u32[]{:S(2)}, u32[]{:S(2)}) collective-permute-start(bf16[128,1,136]{0,2,1:T(8,128)(2,1)S(1)} %get-tuple-element.126), channel_id=1, source_target_pairs={{0,4},{4,8},{8,12},{1,5},{5,9},{9,13},{2,6},{6,10},{10,14},{3,7},{... | collective-permute-start | bytes 104456 | tf_op jit(solution)/shard_map/ppermute | solution.py:19
  93.2 2.8 %copy-start.71 = (pred[128]{0:T(512)(128)(4,1)S(1)}, pred[128]{0:T(512)(128)(4,1)}, u32[]{:S(2)}) copy-start(pred[128]{0:T(512)(128)(4,1)} %copy-done.70) | copy-start | bytes 388
  96.0 1.5 copy-start.42
  98.5 1.5 copy-start.34
  98.8 1.5 copy-start.33
  99.0 1.5 copy-start.32
  99.3 1.5 copy-start.31
  99.5 1.5 copy-start.30
  99.8 1.5 copy-start.29
  100.1 1.5 copy-start.28
  100.3 1.5 copy-start.27
  101.3 1.5 copy-start.23
  101.6 1.5 copy-start.22
  101.8 1.5 copy-start.21
  105.6 114.4 %all-reduce.4.cloned.1.call-start = ((), (), s32[]{:S(2)}) async-start(), calls=%async_computation.2 | async-start | bytes 7077888 | tf_op jit(solution)/shard_map/psum | solution.py:79
  105.9 8.8 %copy-start.6 = (bf16[256,4,128]{0,2,1:T(8,128)(2,1)S(1)}, bf16[256,4,128]{0,2,1:T(8,128)(2,1)}, u32[]{:S(2)}) copy-start(bf16[256,4,128]{0,2,1:T(8,128)(2,1)} %get-tuple-element.81) | copy-start | bytes 786436
  105.9 9.1 %copy-start.1 = (bf16[256,4,128]{0,2,1:T(8,128)(2,1)S(1)}, bf16[256,4,128]{0,2,1:T(8,128)(2,1)}, u32[]{:S(2)}) copy-start(bf16[256,4,128]{0,2,1:T(8,128)(2,1)} %get-tuple-element.68) | copy-start | bytes 786436
  105.9 9.7 %copy-start.3 = (bf16[256,4,128]{0,2,1:T(8,128)(2,1)S(1)}, bf16[256,4,128]{0,2,1:T(8,128)(2,1)}, u32[]{:S(2)}) copy-start(bf16[256,4,128]{0,2,1:T(8,128)(2,1)} %get-tuple-element.80) | copy-start | bytes 786436
  109.7 7.6 %copy-start.12 = (bf16[256,4,128]{0,2,1:T(8,128)(2,1)S(1)}, bf16[256,4,128]{0,2,1:T(8,128)(2,1)}, u32[]{:S(2)}) copy-start(bf16[256,4,128]{0,2,1:T(8,128)(2,1)} %get-tuple-element.78) | copy-start | bytes 786436
  111.0 6.6 %copy-start.9 = (bf16[256,4,128]{0,2,1:T(8,128)(2,1)S(1)}, bf16[256,4,128]{0,2,1:T(8,128)(2,1)}, u32[]{:S(2)}) copy-start(bf16[256,4,128]{0,2,1:T(8,128)(2,1)} %get-tuple-element.71) | copy-start | bytes 786436
  112.2 5.6 %copy-start.8 = (bf16[256,4,128]{0,2,1:T(8,128)(2,1)S(1)}, bf16[256,4,128]{0,2,1:T(8,128)(2,1)}, u32[]{:S(2)}) copy-start(bf16[256,4,128]{0,2,1:T(8,128)(2,1)} %get-tuple-element.86) | copy-start | bytes 786436
  116.5 3.7 %copy-start.10 = (bf16[256,4,128]{0,2,1:T(8,128)(2,1)S(1)}, bf16[256,4,128]{0,2,1:T(8,128)(2,1)}, u32[]{:S(2)}) copy-start(bf16[256,4,128]{0,2,1:T(8,128)(2,1)} %get-tuple-element.66) | copy-start | bytes 786436
  124.9 6.6 %copy-start.44 = (bf16[1,128,256]{2,1,0:T(8,128)(2,1)S(1)}, bf16[1,128,256]{2,1,0:T(8,128)(2,1)}, u32[]{:S(2)}) copy-start(bf16[1,128,256]{2,1,0:T(8,128)(2,1)} %copy.169) | copy-start | bytes 196612
  124.9 8.4 %copy-start.43 = (bf16[1,128,256]{2,1,0:T(8,128)(2,1)S(1)}, bf16[1,128,256]{2,1,0:T(8,128)(2,1)}, u32[]{:S(2)}) copy-start(bf16[1,128,256]{2,1,0:T(8,128)(2,1)} %copy.152) | copy-start | bytes 196612
  133.3 4.7 %copy-start.63 = (bf16[1,128,256]{2,1,0:T(8,128)(2,1)S(1)}, bf16[1,128,256]{2,1,0:T(8,128)(2,1)}, u32[]{:S(2)}) copy-start(bf16[1,128,256]{2,1,0:T(8,128)(2,1)} %copy.155) | copy-start | bytes 196612
  135.3 5.2 %copy-start.5 = (bf16[256,4,128]{0,2,1:T(8,128)(2,1)S(1)}, bf16[256,4,128]{0,2,1:T(8,128)(2,1)}, u32[]{:S(2)}) copy-start(bf16[256,4,128]{0,2,1:T(8,128)(2,1)} %get-tuple-element.67) | copy-start | bytes 786436
  135.3 6.3 %copy-start = (bf16[256,4,128]{0,2,1:T(8,128)(2,1)S(1)}, bf16[256,4,128]{0,2,1:T(8,128)(2,1)}, u32[]{:S(2)}) copy-start(bf16[256,4,128]{0,2,1:T(8,128)(2,1)} %get-tuple-element.90) | copy-start | bytes 786436
  135.3 6.3 %copy-start.62 = (bf16[1,128,256]{2,1,0:T(8,128)(2,1)S(1)}, bf16[1,128,256]{2,1,0:T(8,128)(2,1)}, u32[]{:S(2)}) copy-start(bf16[1,128,256]{2,1,0:T(8,128)(2,1)} %copy.158) | copy-start | bytes 196612
  135.3 6.5 %copy-start.7 = (bf16[256,4,128]{0,2,1:T(8,128)(2,1)S(1)}, bf16[256,4,128]{0,2,1:T(8,128)(2,1)}, u32[]{:S(2)}) copy-start(bf16[256,4,128]{0,2,1:T(8,128)(2,1)} %get-tuple-element.81) | copy-start | bytes 786436
  135.3 6.5 %copy-start.61 = (bf16[1,128,256]{2,1,0:T(8,128)(2,1)S(1)}, bf16[1,128,256]{2,1,0:T(8,128)(2,1)}, u32[]{:S(2)}) copy-start(bf16[1,128,256]{2,1,0:T(8,128)(2,1)} %copy.159) | copy-start | bytes 196612
  135.3 6.8 %copy-start.2 = (bf16[256,4,128]{0,2,1:T(8,128)(2,1)S(1)}, bf16[256,4,128]{0,2,1:T(8,128)(2,1)}, u32[]{:S(2)}) copy-start(bf16[256,4,128]{0,2,1:T(8,128)(2,1)} %get-tuple-element.68) | copy-start | bytes 786436
  135.3 6.8 %copy-start.60 = (bf16[1,128,256]{2,1,0:T(8,128)(2,1)S(1)}, bf16[1,128,256]{2,1,0:T(8,128)(2,1)}, u32[]{:S(2)}) copy-start(bf16[1,128,256]{2,1,0:T(8,128)(2,1)} %copy.160) | copy-start | bytes 196612
  135.3 7.0 %copy-start.59 = (bf16[1,128,256]{2,1,0:T(8,128)(2,1)S(1)}, bf16[1,128,256]{2,1,0:T(8,128)(2,1)}, u32[]{:S(2)}) copy-start(bf16[1,128,256]{2,1,0:T(8,128)(2,1)} %copy.161) | copy-start | bytes 196612
  136.7 5.9 %copy-start.4 = (bf16[256,4,128]{0,2,1:T(8,128)(2,1)S(1)}, bf16[256,4,128]{0,2,1:T(8,128)(2,1)}, u32[]{:S(2)}) copy-start(bf16[256,4,128]{0,2,1:T(8,128)(2,1)} %get-tuple-element.80) | copy-start | bytes 786436
  136.7 5.9 %copy-start.58 = (bf16[1,128,256]{2,1,0:T(8,128)(2,1)S(1)}, bf16[1,128,256]{2,1,0:T(8,128)(2,1)}, u32[]{:S(2)}) copy-start(bf16[1,128,256]{2,1,0:T(8,128)(2,1)} %copy.162) | copy-start | bytes 196612
  138.0 4.9 %copy-start.57 = (bf16[1,128,256]{2,1,0:T(8,128)(2,1)S(1)}, bf16[1,128,256]{2,1,0:T(8,128)(2,1)}, u32[]{:S(2)}) copy-start(bf16[1,128,256]{2,1,0:T(8,128)(2,1)} %copy.163) | copy-start | bytes 196612
  139.2 3.9 %copy-start.56 = (bf16[1,128,256]{2,1,0:T(8,128)(2,1)S(1)}, bf16[1,128,256]{2,1,0:T(8,128)(2,1)}, u32[]{:S(2)}) copy-start(bf16[1,128,256]{2,1,0:T(8,128)(2,1)} %copy.164) | copy-start | bytes 196612
  140.4 2.9 %copy-start.55 = (bf16[1,128,256]{2,1,0:T(8,128)(2,1)S(1)}, bf16[1,128,256]{2,1,0:T(8,128)(2,1)}, u32[]{:S(2)}) copy-start(bf16[1,128,256]{2,1,0:T(8,128)(2,1)} %copy.165) | copy-start | bytes 196612
  141.5 2.1 copy-start.54
  141.8 2.1 copy-start.53
  142.0 2.1 copy-start.13
  142.0 2.1 copy-start.14
  142.0 2.1 copy-start.15
  142.1 2.1 copy-start.65
  142.3 2.0 copy-start.52
  142.6 2.0 copy-start.51
  142.8 2.0 copy-start.50
  143.1 2.0 copy-start.49
  143.3 2.0 copy-start.48
  143.6 2.0 copy-start.47
  143.8 2.0 copy-start.46
  144.1 1.9 copy-start.11
  144.1 1.9 copy-start.45
  (18 other events, 24.7 us)
Sparse Core Ops, SparseCore 0:
  105.8 15.2 reduce-scatter.1
Sparse Core Ops, SparseCore 1:
  135.3 84.6 all-reduce.3
where the time goes:
time: 234 us; the launch traced here: 233 us
  local copies, waits for them, and re-layouts  71.7 us (31%)
  waiting for transfers between devices  71.2 us (30%)
  matrix products  37.1 us (16%)
  starting transfers between devices  21.6 us (9%)
  between operations  17.2 us (7%)
  other arithmetic  7.03 us (3%)
  blocking collectives  6.68 us (3%)
    psum x1, waiting for transfers between devices, body(): weight_grad = lax.psum(local_grad, ('tile', 'sub'))  71.2 us
    slice x29, local copies, waits for them, and re-layouts, body(): columns = by_tap[tap_idx]  41.3 us
    ppermute x4, starting transfers between devices, with_halo(): lax.ppermute(tail, axis, [(i, (i + 1) % count) for i in range(ends)])  16.2 us
    dot_general x27, matrix products, body(): jnp.dot(columns, window, preferred_element_type=jnp.float32)  16 us
    dot_general x27, matrix products, body(): lax.dot_general(grad_flat, window, (((1,), (1,)), ((), ())), preferred_el...  14.1 us
    unnamed x150, local copies, waits for them, and re-layouts  12.9 us
    mul x2, local copies, waits for them, and re-layouts, body(): grad_acc.transpose(1, 2, 0).reshape(local_ch, total_ch * 27) * scale  8.77 us
    dot_general x27, matrix products, body(): jnp.dot(rows_w, window, preferred_element_type=jnp.float32)  6.97 us
  transfers between devices with their start and end apart: 10, of which 1 were waited for; matrix products, arithmetic and copies ran while one was open for 44% of the time, Pallas kernels for 0%

commit v1 on v0

v1 whole, which is shorter than its diff:
```python
import functools
import math

import jax
import jax.numpy as jnp
from jax import lax
from jax.experimental import pallas as pl
from jax.experimental.pallas import tpu as pltpu
from jax.sharding import PartitionSpec as P

ZS = 4
BF = jnp.bfloat16
F32 = jnp.float32
VMEM = pl.BlockSpec(memory_space=pltpu.VMEM)
SMEM = pl.BlockSpec(memory_space=pltpu.SMEM)
PARAMS = pltpu.CompilerParams(vmem_limit_bytes=56 * 2**20)


def cost(flops, bytes_accessed):
    return pl.CostEstimate(flops=flops, bytes_accessed=bytes_accessed, transcendentals=0)


def rotate(x, axis, k):
    n = lax.axis_size(axis)
    if k % n == 0:
        return x
    return lax.ppermute(x, axis, [(i, (i + k) % n) for i in range(n)])


def shifted(v, dy, dz, sub, count):
    lanes = v.shape[-1]
    move = ZS * dy + dz
    if move == 0:
        return v
    turned = pltpu.roll(v, (-move) % lanes, v.ndim - 1)
    lane = lax.broadcasted_iota(jnp.int32, v.shape, v.ndim - 1)
    pos = lane + sub * (lanes // count)
    pos = jnp.where(pos >= lanes, pos - lanes, pos)
    z = pos & (ZS - 1)
    y = pos >> 2
    inside = (z + dz >= 0) & (z + dz < ZS) & (y + dy >= 0) & (y + dy < lanes // ZS)
    return jnp.where(inside, turned, jnp.zeros((), v.dtype))


def filter_kernel(n_chan, ids, w_ref, wt_ref, wn_ref, rows):
    local, columns = w_ref.shape
    total = columns // 27
    mine = ids[1]
    for j in range(columns // 128):
        rows[j * 128 : (j + 1) * 128, :] = w_ref[:, j * 128 : (j + 1) * 128].astype(F32).T
    for t in range(27):
        for j in range(n_chan):
            true = lax.rem(mine + j, n_chan)
            v = rows[pl.ds(true * (local * 27) + t, local, stride=27), :]
            wt_ref[j * local : (j + 1) * local, t * local : (t + 1) * local] = v.astype(BF)
            at = t * total + j * local
            wn_ref[:, at : at + local] = v.T.astype(BF)


def conv_kernel(n_chan, n_sub, n_tile, ids, *refs):
    n_act = 3 * n_chan * n_sub
    acts, grads = refs[:n_act], refs[n_act : n_act + 3 * n_sub]
    wt_ref, wn_ref = refs[n_act + 3 * n_sub : n_act + 3 * n_sub + 2]
    conv_ref = refs[n_act + 3 * n_sub + 2]
    part_refs = refs[n_act + 3 * n_sub + 3 : n_act + 3 * n_sub + 3 + n_chan]
    act_cols, grad_cols = refs[-2:]
    planes, local, span = acts[0].shape
    total = n_chan * local
    tile, sub = ids[0], ids[2]

    def plane(group, x):
        if x == 0:
            v = jnp.concatenate([r[planes - 1] for r in group[1]], axis=1)
            return jnp.where(tile > 0, v, jnp.zeros((), BF))
        if x == planes + 1:
            v = jnp.concatenate([r[0] for r in group[2]], axis=1)
            return jnp.where(tile < n_tile - 1, v, jnp.zeros((), BF))
        return jnp.concatenate([r[x - 1] for r in group[0]], axis=1)

    for j in range(n_chan):
        group = [[acts[(b * n_chan + j) * n_sub + u] for u in range(n_sub)] for b in range(3)]
        for x in range(planes + 2):
            v = plane(group, x)
            for bc in range(9):
                s = shifted(v, bc // 3 - 1, bc % 3 - 1, sub, n_sub)
                at = bc * total + j * local
                act_cols[at : at + local, x * span : (x + 1) * span] = s[:, :span]
    group = [[grads[b * n_sub + u] for u in range(n_sub)] for b in range(3)]
    for x in range(planes + 2):
        v = plane(group, x)
        for bc in range(9):
            s = shifted(v, 1 - bc // 3, 1 - bc % 3, sub, n_sub)
            grad_cols[bc * local : (bc + 1) * local, x * span : (x + 1) * span] = s[:, :span]
    cells = planes * span
    out = jnp.zeros((local, cells), F32)
    for a in range(3):
        out += jnp.dot(
            wn_ref[:, a * 9 * total : (a + 1) * 9 * total],
            act_cols[:, a * span : a * span + cells],
            preferred_element_type=F32,
        )
    for x in range(planes):
        conv_ref[:, x, :] = out[:, x * span : (x + 1) * span].astype(BF)
    for j in range(n_chan):
        part = jnp.zeros((local, cells), F32)
        for a in range(3):
            part += jnp.dot(
                wt_ref[j * local : (j + 1) * local, a * 9 * local : (a + 1) * 9 * local],
                grad_cols[:, (2 - a) * span : (2 - a) * span + cells],
                preferred_element_type=F32,
            )
        part_refs[j][...] = part


def update_kernel(n_chan, n_sub, n_tile, scale, ids, *refs):
    n_act = n_tile * n_chan * n_sub
    acts, grads = refs[:n_act], refs[n_act : n_act + n_tile * n_sub]
    parts = refs[n_act + n_tile * n_sub : n_act + n_tile * n_sub + n_chan]
    out_ref, ig_ref, act_all, grad_all, rows = refs[-5:]
    planes, local, span = acts[0].shape
    wide = span * n_sub
    depth = n_tile * planes * wide
    total = n_chan * local
    tile, mine, sub = ids[0], ids[1], ids[2]
    act_all[:, :wide] = jnp.zeros((total, wide), BF)
    act_all[:, depth + wide :] = jnp.zeros((total, wide), BF)
    for k in range(n_tile):
        first = lax.rem(tile - k + n_tile, n_tile) * planes
        for x in range(planes):
            at = pl.multiple_of((first + x) * wide, wide)
            for j in range(n_chan):
                for u in range(n_sub):
                    act_all[
                        j * local : (j + 1) * local,
                        pl.ds(pl.multiple_of(at + wide + u * span, span), span),
                    ] = acts[(k * n_chan + j) * n_sub + u][x]
            v = jnp.concatenate([grads[k * n_sub + u][x] for u in range(n_sub)], axis=1)
            for bc in range(9):
                grad_all[bc * local : (bc + 1) * local, pl.ds(at, wide)] = shifted(
                    v, 1 - bc // 3, 1 - bc % 3, sub, n_sub
                )
    ig = parts[0][...]
    for j in range(1, n_chan):
        ig = ig + parts[j][...]
    for x in range(planes):
        ig_ref[:, x, :] = ig[:, x * span : (x + 1) * span].astype(BF)
    group = max(1, 256 // local)

    def taps(a, carry):
        lhs = act_all[:, pl.ds(pl.multiple_of(a * wide, wide), depth)]
        for p in range(0, 9, group):
            n = min(group, 9 - p)
            r = lax.dot_general(
                lhs,
                grad_all[p * local : (p + n) * local, :],
                (((1,), (1,)), ((), ())),
                preferred_element_type=F32,
            )
            for i in range(n):
                for j in range(n_chan):
                    true = lax.rem(mine + j, n_chan)
                    start = true * (local * 27) + a * 9 + p + i
                    rows[pl.ds(start, local, stride=27), :] = r[
                        j * local : (j + 1) * local, i * local : (i + 1) * local
                    ]
        return carry

    lax.fori_loop(0, 3, taps, 0)
    for j in range(total * 27 // 128):
        out_ref[:, j * 128 : (j + 1) * 128] = rows[j * 128 : (j + 1) * 128, :].T * scale


def body(activations, out_grad, weight):
    local, planes, span = activations.shape
    n_tile, n_chan, n_sub = (lax.axis_size(a) for a in ("tile", "chan", "sub"))
    total = weight.shape[1] // 27
    cells = planes * span
    scale = 1.0 / math.sqrt(cells * n_tile * n_sub)
    ids = jnp.stack([lax.axis_index(a) for a in ("tile", "chan", "sub")]).astype(jnp.int32)
    act = activations.transpose(1, 0, 2)
    grad = out_grad.transpose(1, 0, 2)
    order = [0, 1, n_tile - 1] + list(range(2, n_tile - 1))
    acts = {k: rotate(act, "tile", k) for k in order}
    grads = {k: rotate(grad, "tile", k) for k in order}
    acts = {(k, j): rotate(acts[k], "chan", -j) for k in order for j in range(n_chan)}
    acts = {(k, j, u): rotate(acts[k, j], "sub", -u) for k, j in acts for u in range(n_sub)}
    grads = {(k, u): rotate(grads[k], "sub", -u) for k in order for u in range(n_sub)}

    wt, wn = pl.pallas_call(
        functools.partial(filter_kernel, n_chan),
        out_shape=(
            jax.ShapeDtypeStruct((total, 27 * local), BF),
            jax.ShapeDtypeStruct((local, 27 * total), BF),
        ),
        in_specs=[SMEM, VMEM],
        out_specs=(VMEM, VMEM),
        scratch_shapes=[pltpu.VMEM((total * 27, local), F32)],
        compiler_params=PARAMS,
        cost_estimate=cost(0, 12 * local * total * 27),
    )(ids, weight)

    near = order[:3]
    conv_in = [acts[k, j, u] for k in near for j in range(n_chan) for u in range(n_sub)]
    conv_in += [grads[k, u] for k in near for u in range(n_sub)]
    conv_out, *parts = pl.pallas_call(
        functools.partial(conv_kernel, n_chan, n_sub, n_tile),
        out_shape=[jax.ShapeDtypeStruct((local, planes, span), BF)]
        + [jax.ShapeDtypeStruct((local, cells), F32)] * n_chan,
        in_specs=[SMEM] + [VMEM] * (len(conv_in) + 2),
        out_specs=[VMEM] * (n_chan + 1),
        scratch_shapes=[
            pltpu.VMEM((9 * total, (planes + 2) * span), BF),
            pltpu.VMEM((9 * local, (planes + 2) * span), BF),
        ],
        compiler_params=PARAMS,
        cost_estimate=cost(4 * 27 * local * total * cells, 4 * 2**20),
    )(ids, *conv_in, wt, wn)
    parts = [rotate(part, "chan", j) for j, part in enumerate(parts)]

    update_in = [acts[k, j, u] for k in range(n_tile) for j in range(n_chan) for u in range(n_sub)]
    update_in += [grads[k, u] for k in range(n_tile) for u in range(n_sub)]
    depth = n_tile * planes * span * n_sub
    weight_grad, input_grad = pl.pallas_call(
        functools.partial(update_kernel, n_chan, n_sub, n_tile, scale),
        out_shape=(
            jax.ShapeDtypeStruct((local, total * 27), F32),
            jax.ShapeDtypeStruct((local, planes, span), BF),
        ),
        in_specs=[SMEM] + [VMEM] * (len(update_in) + n_chan),
        out_specs=(VMEM, VMEM),
        scratch_shapes=[
            pltpu.VMEM((total, depth + 2 * span * n_sub), BF),
            pltpu.VMEM((9 * local, depth), BF),
            pltpu.VMEM((total * 27, local), F32),
        ],
        compiler_params=PARAMS,
        cost_estimate=cost(2 * 27 * local * total * depth, 8 * 2**20),
    )(ids, *update_in, *parts)
    return conv_out, input_grad, weight_grad


def solution(mesh):
    placed = (
        P("chan", ("groups", "tile"), "sub"),
        P("chan", ("groups", "tile"), "sub"),
        P("chan", None),
    )
    return jax.shard_map(
        body,
        mesh=mesh,
        in_specs=placed,
        out_specs=(
            P("chan", ("groups", "tile"), "sub"),
            P("chan", ("groups", "tile"), "sub"),
            P(("groups", "chan"), None),
        ),
        check_vma=False,
    )
```

time: 234 us -> 75.6 us (0.32)
  local copies, waits for them, and re-layouts: 71.7 us -> 3.16 us
  waiting for transfers between devices: 71.2 us -> 20.1 us
  matrix products: 37.1 us -> 0 us
  Pallas kernels: 0 us -> 29.3 us
  between operations: 17.2 us -> 1.05 us
  blocking collectives: 6.68 us -> 0 us
  other arithmetic: 7.03 us -> 0.6 us
    psum x1 -> x0, waiting for transfers between devices: 71.2 us -> none  [body(): weight_grad = lax.psum(local_grad, ('tile', 'sub'))]
    slice x33 -> x0, local copies, waits for them, and re-layouts: 47.5 us -> none  [the longest x29 41.3 us: body(): columns = by_tap[tap_idx]]
    dot_general x81 -> x0, matrix products: 37.1 us -> none  [the longest x27 16 us: body(): jnp.dot(columns, window, preferred_element_type=jnp.float32)]
    pallas_call x0 -> x3, Pallas kernels: none -> 29.3 us  [the longest x1 17.1 us: body(): pl.pallas_call(functools.partial(update_kernel, n_chan, n_sub, n_tile, sc...]
    ppermute x8 -> x23, waiting for transfers between devices: 0.02 us -> 20.1 us  [rotate(): return lax.ppermute(x, axis, [(i, (i + k) % n) for i in range(n)])]
    unnamed x150 -> x52, local copies, waits for them, and re-layouts: 12.9 us -> 3.16 us
    mul x2 -> x0, local copies, waits for them, and re-layouts: 8.77 us -> none  [body(): grad_acc.transpose(1, 2, 0).reshape(local_ch, total_ch * 27) * scale]
    all_gather x1 -> x0, blocking collectives: 6.68 us -> none  [body(): piece = lax.all_gather(padded_x, 'chan', axis=0, tiled=True)]
  transfers between devices with their start and end apart: 10 -> 23, of which waited for: 1 -> 8; matrix products, arithmetic and copies ran while one was open for 44% -> 2% of each run, Pallas kernels for 0% -> 16%
where the time goes in v1:
time: 75.6 us; the launch traced here: 75.4 us
  Pallas kernels  29.3 us (39%)
  starting transfers between devices  21.1 us (28%)
  waiting for transfers between devices  20.1 us (27%)
  local copies, waits for them, and re-layouts  3.16 us (4%)
  between operations  1.05 us (1%)
    ppermute x23, starting transfers between devices, rotate(): return lax.ppermute(x, axis, [(i, (i + k) % n) for i in range(n)])  21.1 us
    ppermute x23, waiting for transfers between devices, rotate(): return lax.ppermute(x, axis, [(i, (i + k) % n) for i in range(n)])  20.1 us
    pallas_call x1, Pallas kernels, body(): pl.pallas_call(functools.partial(update_kernel, n_chan, n_sub, n_tile, sc...  17.1 us
    pallas_call x1, Pallas kernels, body(): pl.pallas_call(functools.partial(conv_kernel, n_chan, n_sub, n_tile), out...  7.62 us
    pallas_call x1, Pallas kernels, body(): pl.pallas_call(functools.partial(filter_kernel, n_chan), out_shape=(jax.S...  4.61 us
    unnamed x52, local copies, waits for them, and re-layouts  3.16 us
  transfers between devices with their start and end apart: 23, of which 8 were waited for; matrix products, arithmetic and copies ran while one was open for 2% of the time, Pallas kernels for 16%

profile of v1, /device:TPU:0, one launch (start us, length us, event | category | flops | bytes accessed | tf_op | source)
XLA Modules:
  0.0 75.4 jit_solution(13916460537174323744)
XLA Ops:
  0.6 0.9 %copy.10 = bf16[128,4,128]{2,0,1:T(8,128)(2,1)S(1)} copy(bf16[128,4,128]{2,1,0:T(4,128)(2,1)} %param.4) | data formatting | bytes 262144 | tf_op args[1]
  1.6 0.0 copy-start
  1.6 5.1 %collective-permute-start.14 = (bf16[4,128,128]{2,1,0:T(8,128)(2,1)S(1)}, bf16[4,128,128]{2,1,0:T(8,128)(2,1)S(1)}, u32[]{:S(2)}, u32[]{:S(2)}) collective-permute-start(bf16[4,128,128]{2,1,0:T(8,128)(2,1)S(1)} %bitcast.9), channel_id=1, source_target_pairs={{0,12},{4,0},{8,4},{12,8},{1,13},{5,1},{9,5},{13,9},{2,14},{6,2},{... | collective-permute-start | bytes 393224 | tf_op jit(solution)/shard_map/ppermute | solution.py:27
  6.7 0.0 collective-permute-start.12
  6.7 0.0 collective-permute-start.11
  6.7 0.9 %copy.11 = bf16[128,4,128]{2,0,1:T(8,128)(2,1)S(1)} copy(bf16[128,4,128]{2,1,0:T(4,128)(2,1)} %param.3) | data formatting | bytes 262144 | tf_op args[0]
  7.6 0.0 copy-start.1
  7.6 1.1 %collective-permute-start.16 = (bf16[4,128,128]{2,1,0:T(8,128)(2,1)S(1)}, bf16[4,128,128]{2,1,0:T(8,128)(2,1)S(1)}, u32[]{:S(2)}, u32[]{:S(2)}) collective-permute-start(bf16[4,128,128]{2,1,0:T(8,128)(2,1)S(1)} %bitcast.15), channel_id=1, source_target_pairs={{0,8},{4,12},{8,0},{12,4},{1,9},{5,13},{9,1},{13,5},{2,10},{6,14},... | collective-permute-start | bytes 393224 | tf_op jit(solution)/shard_map/ppermute | solution.py:27
  8.7 2.9 %collective-permute-start.7 = (bf16[4,128,128]{2,1,0:T(8,128)(2,1)S(1)}, bf16[4,128,128]{2,1,0:T(8,128)(2,1)S(1)}, u32[]{:S(2)}, u32[]{:S(2)}) collective-permute-start(bf16[4,128,128]{2,1,0:T(8,128)(2,1)S(1)} %bitcast.16), channel_id=1, source_target_pairs={{0,12},{4,0},{8,4},{12,8},{1,13},{5,1},{9,5},{13,9},{2,14},{6,2},{... | collective-permute-start | bytes 393224 | tf_op jit(solution)/shard_map/ppermute | solution.py:27
  11.6 0.0 collective-permute-done.14.refs_16_.refs_22_
  11.6 0.6 collective-permute-start.3
  12.1 2.0 %collective-permute-done.12.refs_14_.refs_18_ = bf16[4,128,128]{2,1,0:T(8,128)(2,1)S(1)} collective-permute-done((bf16[4,128,128]{2,1,0:T(8,128)(2,1)S(1)}, bf16[4,128,128]{2,1,0:T(8,128)(2,1)S(1)}, u32[]{:S(2)}, u32[]{:S(2)}) %collective-permute-start.12) | collective-permute-done | bytes 131104 | tf_op jit(solution)/shard_map/ppermute | solution.py:27
  14.1 1.5 %collective-permute-start.1 = (bf16[4,128,128]{2,1,0:T(8,128)(2,1)S(1)}, bf16[4,128,128]{2,1,0:T(8,128)(2,1)S(1)}, u32[]{:S(2)}, u32[]{:S(2)}) collective-permute-start(bf16[4,128,128]{2,1,0:T(8,128)(2,1)S(1)} %bitcast.18), channel_id=1, source_target_pairs={{0,2},{2,0},{1,3},{3,1},{4,6},{6,4},{5,7},{7,5},{8,10},{10,8},{9,1... | collective-permute-start | bytes 393224 | tf_op jit(solution)/shard_map/ppermute | solution.py:27
  15.6 0.0 collective-permute-done.11.refs_13_.refs_17_
  15.6 0.0 collective-permute-start
  15.6 4.1 %collective-permute-done.16.refs_8_ = bf16[4,128,128]{2,1,0:T(8,128)(2,1)S(1)} collective-permute-done((bf16[4,128,128]{2,1,0:T(8,128)(2,1)S(1)}, bf16[4,128,128]{2,1,0:T(8,128)(2,1)S(1)}, u32[]{:S(2)}, u32[]{:S(2)}) %collective-permute-start.16) | collective-permute-done | bytes 131104 | tf_op jit(solution)/shard_map/ppermute | solution.py:27
  19.8 0.0 collective-permute-start.15
  19.8 0.0 collective-permute-done.7.refs_8_.refs_12_
  19.8 0.0 copy-start.7
  19.8 0.5 collective-permute-start.13
  20.3 1.7 %collective-permute-done.3.refs_4_ = bf16[4,128,128]{2,1,0:T(8,128)(2,1)S(1)} collective-permute-done((bf16[4,128,128]{2,1,0:T(8,128)(2,1)S(1)}, bf16[4,128,128]{2,1,0:T(8,128)(2,1)S(1)}, u32[]{:S(2)}, u32[]{:S(2)}) %collective-permute-start.3) | collective-permute-done | bytes 131104 | tf_op jit(solution)/shard_map/ppermute | solution.py:27
  22.0 1.5 %collective-permute-start.9 = (bf16[4,128,128]{2,1,0:T(8,128)(2,1)S(1)}, bf16[4,128,128]{2,1,0:T(8,128)(2,1)S(1)}, u32[]{:S(2)}, u32[]{:S(2)}) collective-permute-start(bf16[4,128,128]{2,1,0:T(8,128)(2,1)S(1)} %collective-permute-done.7.refs_8_.refs_12_), channel_id=1, source_target_pairs={{0,2},{2,0},{1,3},{3,1},{4,6},{6,4},{5,7},{7,5},{8,10},{10,8},{9,1... | collective-permute-start | bytes 393224 | tf_op jit(solution)/shard_map/ppermute | solution.py:27
  23.5 0.0 collective-permute-done.1.refs_2_
  23.5 0.5 collective-permute-start.5
  24.0 0.0 collective-permute-done.refs_1_
  24.0 0.0 collective-permute-start.8
  24.0 0.0 collective-permute-done.15.refs_17_.refs_23_
  24.1 0.0 copy-start.11
  24.1 0.5 collective-permute-start.4
  24.6 0.0 collective-permute-done.13.refs_15_.refs_19_
  24.6 0.1 collective-permute-start.2
  24.6 3.6 %collective-permute-done.9.refs_10_.refs_14_ = bf16[4,128,128]{2,1,0:T(8,128)(2,1)S(1)} collective-permute-done((bf16[4,128,128]{2,1,0:T(8,128)(2,1)S(1)}, bf16[4,128,128]{2,1,0:T(8,128)(2,1)S(1)}, u32[]{:S(2)}, u32[]{:S(2)}) %collective-permute-start.9) | collective-permute-done | bytes 131104 | tf_op jit(solution)/shard_map/ppermute | solution.py:27
  28.3 0.0 collective-permute-start.10
  28.3 1.4 %collective-permute-done.5.refs_6_ = bf16[4,128,128]{2,1,0:T(8,128)(2,1)S(1)} collective-permute-done((bf16[4,128,128]{2,1,0:T(8,128)(2,1)S(1)}, bf16[4,128,128]{2,1,0:T(8,128)(2,1)S(1)}, u32[]{:S(2)}, u32[]{:S(2)}) %collective-permute-start.5) | collective-permute-done | bytes 131104 | tf_op jit(solution)/shard_map/ppermute | solution.py:27
  29.7 0.0 collective-permute-start.6
  29.7 0.6 pad_add_fusion.ids
  30.3 4.6 %shard_map.58 = (bf16[256,3456]{1,0:T(8,128)(2,1)}, bf16[128,6912]{1,0:T(8,128)(2,1)}) custom-call(s32[3]{0:T(128)} %pad_add_fusion.ids, bf16[128,6912]{1,0:T(8,128)(2,1)} %w_ref.1), custom_call_target="tpu_custom_call" | custom-call | bytes 10616832 | tf_op jit(solution)/shard_map/pallas_call | solution.py:189
  34.9 0.0 collective-permute-done.8.refs_9_.refs_13_
  34.9 4.3 %collective-permute-start.20 = (bf16[4,128,128]{2,1,0:T(8,128)(2,1)S(1)}, bf16[4,128,128]{2,1,0:T(8,128)(2,1)S(1)}, u32[]{:S(2)}, u32[]{:S(2)}) collective-permute-start(bf16[4,128,128]{2,1,0:T(8,128)(2,1)S(1)} %bitcast.12), channel_id=1, source_target_pairs={{0,8},{4,12},{8,0},{12,4},{1,9},{5,13},{9,1},{13,5},{2,10},{6,14},... | collective-permute-start | bytes 393224 | tf_op jit(solution)/shard_map/ppermute | solution.py:27
  39.2 0.0 collective-permute-done.4.refs_5_
  39.2 1.5 %collective-permute-start.18 = (bf16[4,128,128]{2,1,0:T(8,128)(2,1)S(1)}, bf16[4,128,128]{2,1,0:T(8,128)(2,1)S(1)}, u32[]{:S(2)}, u32[]{:S(2)}) collective-permute-start(bf16[4,128,128]{2,1,0:T(8,128)(2,1)S(1)} %collective-permute-done.16.refs_8_), channel_id=1, source_target_pairs={{0,2},{2,0},{1,3},{3,1},{4,6},{6,4},{5,7},{7,5},{8,10},{10,8},{9,1... | collective-permute-start | bytes 393224 | tf_op jit(solution)/shard_map/ppermute | solution.py:27
  40.7 0.0 collective-permute-done.2.refs_3_
  40.7 0.0 collective-permute-done.10.refs_11_.refs_15_
  40.7 0.0 copy-start.18
  40.7 0.0 collective-permute-done.6.refs_7_
  40.9 0.5 copy-done.17
  41.3 0.1 copy-done.18
  41.4 0.0 copy-done.19
  41.4 7.6 %shard_map.59 = (bf16[128,4,128]{2,1,0:T(4,128)(2,1)}, f32[128,512]{1,0:T(8,128)}, f32[128,512]{1,0:T(8,128)}) custom-call(s32[3]{0:T(128)} %pad_add_fusion.ids, bf16[4,128,128]{2,1,0:T(8,128)(2,1)} %bitcast.20, bf16[4,128,128]{2,1,0:T(8,128)(2,1)} %copy-done.10, bf16[4,128,128]{2,1,0:T(8,128)(2,1)} %copy-done.9, bf16[4,128,128]{2,1,0:T(8,128)(2,1)} %copy-done.17, ...), custom_call_target="tpu_custom_call" | custom-call | flops 1811939328 | bytes 4194304 | tf_op jit(solution)/shard_map/pallas_call | solution.py:205
  49.0 0.5 collective-permute-start.22
  49.6 0.0 collective-permute-start.17
  49.6 0.0 collective-permute-done.20.refs_20_
  49.6 0.5 collective-permute-start.21
  50.1 0.0 collective-permute-done.18.refs_10_
  50.1 0.1 collective-permute-start.19
  50.2 0.9 %collective-permute-done.21.refs_21_ = bf16[4,128,128]{2,1,0:T(8,128)(2,1)S(1)} collective-permute-done((bf16[4,128,128]{2,1,0:T(8,128)(2,1)S(1)}, bf16[4,128,128]{2,1,0:T(8,128)(2,1)S(1)}, u32[]{:S(2)}, u32[]{:S(2)}) %collective-permute-start.21) | collective-permute-done | bytes 131104 | tf_op jit(solution)/shard_map/ppermute | solution.py:27
  51.1 0.0 collective-permute-done.17.refs_9_
  51.1 0.3 collective-permute-done.19.refs_11_
  51.4 6.0 %collective-permute-done.22.refs_25_ = f32[128,512]{1,0:T(8,128)S(1)} collective-permute-done((f32[128,512]{1,0:T(8,128)}, f32[128,512]{1,0:T(8,128)S(1)}, u32[]{:S(2)}, u32[]{:S(2)}) %collective-permute-start.22) | collective-permute-done | bytes 262176 | tf_op jit(solution)/shard_map/ppermute | solution.py:27
  57.4 0.0 copy-done.21
  57.4 0.0 copy-done.22
  57.4 0.0 copy-done.24
  57.4 0.7 copy-done.2
  58.1 17.1 %shard_map.60 = (f32[128,6912]{1,0:T(8,128)}, bf16[128,4,128]{2,1,0:T(4,128)(2,1)}) custom-call(s32[3]{0:T(128)} %pad_add_fusion.ids, bf16[4,128,128]{2,1,0:T(8,128)(2,1)} %bitcast.21, bf16[4,128,128]{2,1,0:T(8,128)(2,1)} %copy-done.10, bf16[4,128,128]{2,1,0:T(8,128)(2,1)} %copy-done.9, bf16[4,128,128]{2,1,0:T(8,128)(2,1)} %copy-done.17, ...), custom_call_target="tpu_custom_call" | custom-call | flops 7247757312 | bytes 8388608 | tf_op jit(solution)/shard_map/pallas_call | solution.py:223
  (38 shorter events, 0.1 us)
Async XLA Ops:
  1.6 39.2 %copy-start = (bf16[128,4,128]{2,0,1:T(8,128)(2,1)}, bf16[128,4,128]{2,0,1:T(8,128)(2,1)S(1)}, u32[]{:S(2)}) copy-start(bf16[128,4,128]{2,0,1:T(8,128)(2,1)S(1)} %copy.10) | copy-start | bytes 393220
  1.6 10.0 %collective-permute-start.14 = (bf16[4,128,128]{2,1,0:T(8,128)(2,1)S(1)}, bf16[4,128,128]{2,1,0:T(8,128)(2,1)S(1)}, u32[]{:S(2)}, u32[]{:S(2)}) collective-permute-start(bf16[4,128,128]{2,1,0:T(8,128)(2,1)S(1)} %bitcast.9), channel_id=1, source_target_pairs={{0,12},{4,0},{8,4},{12,8},{1,13},{5,1},{9,5},{13,9},{2,14},{6,2},{... | collective-permute-start | bytes 393224 | tf_op jit(solution)/shard_map/ppermute | solution.py:27
  6.7 7.5 %collective-permute-start.12 = (bf16[4,128,128]{2,1,0:T(8,128)(2,1)S(1)}, bf16[4,128,128]{2,1,0:T(8,128)(2,1)S(1)}, u32[]{:S(2)}, u32[]{:S(2)}) collective-permute-start(bf16[4,128,128]{2,1,0:T(8,128)(2,1)S(1)} %bitcast.10), channel_id=1, source_target_pairs={{0,4},{4,8},{8,12},{12,0},{1,5},{5,9},{9,13},{13,1},{2,6},{6,10},{... | collective-permute-start | bytes 393224 | tf_op jit(solution)/shard_map/ppermute | solution.py:27
  6.7 9.0 %collective-permute-start.11 = (bf16[4,128,128]{2,1,0:T(8,128)(2,1)S(1)}, bf16[4,128,128]{2,1,0:T(8,128)(2,1)S(1)}, u32[]{:S(2)}, u32[]{:S(2)}) collective-permute-start(bf16[4,128,128]{2,1,0:T(8,128)(2,1)S(1)} %bitcast.11), channel_id=1, source_target_pairs={{0,1},{1,0},{2,3},{3,2},{4,5},{5,4},{6,7},{7,6},{8,9},{9,8},{10,11... | collective-permute-start | bytes 393224 | tf_op jit(solution)/shard_map/ppermute | solution.py:27
  7.6 33.1 %copy-start.1 = (bf16[128,4,128]{2,0,1:T(8,128)(2,1)}, bf16[128,4,128]{2,0,1:T(8,128)(2,1)S(1)}, u32[]{:S(2)}) copy-start(bf16[128,4,128]{2,0,1:T(8,128)(2,1)S(1)} %copy.11) | copy-start | bytes 393220
  7.6 12.2 %collective-permute-start.16 = (bf16[4,128,128]{2,1,0:T(8,128)(2,1)S(1)}, bf16[4,128,128]{2,1,0:T(8,128)(2,1)S(1)}, u32[]{:S(2)}, u32[]{:S(2)}) collective-permute-start(bf16[4,128,128]{2,1,0:T(8,128)(2,1)S(1)} %bitcast.15), channel_id=1, source_target_pairs={{0,8},{4,12},{8,0},{12,4},{1,9},{5,13},{9,1},{13,5},{2,10},{6,14},... | collective-permute-start | bytes 393224 | tf_op jit(solution)/shard_map/ppermute | solution.py:27
  8.7 11.1 %collective-permute-start.7 = (bf16[4,128,128]{2,1,0:T(8,128)(2,1)S(1)}, bf16[4,128,128]{2,1,0:T(8,128)(2,1)S(1)}, u32[]{:S(2)}, u32[]{:S(2)}) collective-permute-start(bf16[4,128,128]{2,1,0:T(8,128)(2,1)S(1)} %bitcast.16), channel_id=1, source_target_pairs={{0,12},{4,0},{8,4},{12,8},{1,13},{5,1},{9,5},{13,9},{2,14},{6,2},{... | collective-permute-start | bytes 393224 | tf_op jit(solution)/shard_map/ppermute | solution.py:27
  11.6 29.2 %copy-start.3 = (bf16[4,128,128]{2,1,0:T(8,128)(2,1)}, bf16[4,128,128]{2,1,0:T(8,128)(2,1)S(1)}, u32[]{:S(2)}) copy-start(bf16[4,128,128]{2,1,0:T(8,128)(2,1)S(1)} %collective-permute-done.14.refs_16_.refs_22_) | copy-start | bytes 393220
  11.6 10.4 %collective-permute-start.3 = (bf16[4,128,128]{2,1,0:T(8,128)(2,1)S(1)}, bf16[4,128,128]{2,1,0:T(8,128)(2,1)S(1)}, u32[]{:S(2)}, u32[]{:S(2)}) collective-permute-start(bf16[4,128,128]{2,1,0:T(8,128)(2,1)S(1)} %bitcast.17), channel_id=1, source_target_pairs={{0,4},{4,8},{8,12},{12,0},{1,5},{5,9},{9,13},{13,1},{2,6},{6,10},{... | collective-permute-start | bytes 393224 | tf_op jit(solution)/shard_map/ppermute | solution.py:27
  14.1 26.6 %copy-start.4 = (bf16[4,128,128]{2,1,0:T(8,128)(2,1)}, bf16[4,128,128]{2,1,0:T(8,128)(2,1)S(1)}, u32[]{:S(2)}) copy-start(bf16[4,128,128]{2,1,0:T(8,128)(2,1)S(1)} %collective-permute-done.12.refs_14_.refs_18_) | copy-start | bytes 393220
  14.1 9.4 %collective-permute-start.1 = (bf16[4,128,128]{2,1,0:T(8,128)(2,1)S(1)}, bf16[4,128,128]{2,1,0:T(8,128)(2,1)S(1)}, u32[]{:S(2)}, u32[]{:S(2)}) collective-permute-start(bf16[4,128,128]{2,1,0:T(8,128)(2,1)S(1)} %bitcast.18), channel_id=1, source_target_pairs={{0,2},{2,0},{1,3},{3,1},{4,6},{6,4},{5,7},{7,5},{8,10},{10,8},{9,1... | collective-permute-start | bytes 393224 | tf_op jit(solution)/shard_map/ppermute | solution.py:27
  15.6 25.1 %copy-start.5 = (bf16[4,128,128]{2,1,0:T(8,128)(2,1)}, bf16[4,128,128]{2,1,0:T(8,128)(2,1)S(1)}, u32[]{:S(2)}) copy-start(bf16[4,128,128]{2,1,0:T(8,128)(2,1)S(1)} %collective-permute-done.11.refs_13_.refs_17_) | copy-start | bytes 393220
  15.6 8.4 %collective-permute-start = (bf16[4,128,128]{2,1,0:T(8,128)(2,1)S(1)}, bf16[4,128,128]{2,1,0:T(8,128)(2,1)S(1)}, u32[]{:S(2)}, u32[]{:S(2)}) collective-permute-start(bf16[4,128,128]{2,1,0:T(8,128)(2,1)S(1)} %bitcast.19), channel_id=1, source_target_pairs={{0,1},{1,0},{2,3},{3,2},{4,5},{5,4},{6,7},{7,6},{8,9},{9,8},{10,11... | collective-permute-start | bytes 393224 | tf_op jit(solution)/shard_map/ppermute | solution.py:27
  19.8 29.8 %copy-start.6 = (bf16[4,128,128]{2,1,0:T(8,128)(2,1)}, bf16[4,128,128]{2,1,0:T(8,128)(2,1)S(1)}, u32[]{:S(2)}) copy-start(bf16[4,128,128]{2,1,0:T(8,128)(2,1)S(1)} %collective-permute-done.16.refs_8_) | copy-start | bytes 393220
  19.8 4.3 %collective-permute-start.15 = (bf16[4,128,128]{2,1,0:T(8,128)(2,1)S(1)}, bf16[4,128,128]{2,1,0:T(8,128)(2,1)S(1)}, u32[]{:S(2)}, u32[]{:S(2)}) collective-permute-start(bf16[4,128,128]{2,1,0:T(8,128)(2,1)S(1)} %collective-permute-done.14.refs_16_.refs_22_), channel_id=1, source_target_pairs={{0,1},{1,0},{2,3},{3,2},{4,5},{5,4},{6,7},{7,6},{8,9},{9,8},{10,11... | collective-permute-start | bytes 393224 | tf_op jit(solution)/shard_map/ppermute | solution.py:27
  19.8 21.0 %copy-start.7 = (bf16[4,128,128]{2,1,0:T(8,128)(2,1)}, bf16[4,128,128]{2,1,0:T(8,128)(2,1)S(1)}, u32[]{:S(2)}) copy-start(bf16[4,128,128]{2,1,0:T(8,128)(2,1)S(1)} %collective-permute-done.7.refs_8_.refs_12_) | copy-start | bytes 393220
  19.8 4.8 %collective-permute-start.13 = (bf16[4,128,128]{2,1,0:T(8,128)(2,1)S(1)}, bf16[4,128,128]{2,1,0:T(8,128)(2,1)S(1)}, u32[]{:S(2)}, u32[]{:S(2)}) collective-permute-start(bf16[4,128,128]{2,1,0:T(8,128)(2,1)S(1)} %collective-permute-done.12.refs_14_.refs_18_), channel_id=1, source_target_pairs={{0,1},{1,0},{2,3},{3,2},{4,5},{5,4},{6,7},{7,6},{8,9},{9,8},{10,11... | collective-permute-start | bytes 393224 | tf_op jit(solution)/shard_map/ppermute | solution.py:27
  22.0 18.8 %copy-start.8 = (bf16[4,128,128]{2,1,0:T(8,128)(2,1)}, bf16[4,128,128]{2,1,0:T(8,128)(2,1)S(1)}, u32[]{:S(2)}) copy-start(bf16[4,128,128]{2,1,0:T(8,128)(2,1)S(1)} %collective-permute-done.3.refs_4_) | copy-start | bytes 393220
  22.0 6.3 %collective-permute-start.9 = (bf16[4,128,128]{2,1,0:T(8,128)(2,1)S(1)}, bf16[4,128,128]{2,1,0:T(8,128)(2,1)S(1)}, u32[]{:S(2)}, u32[]{:S(2)}) collective-permute-start(bf16[4,128,128]{2,1,0:T(8,128)(2,1)S(1)} %collective-permute-done.7.refs_8_.refs_12_), channel_id=1, source_target_pairs={{0,2},{2,0},{1,3},{3,1},{4,6},{6,4},{5,7},{7,5},{8,10},{10,8},{9,1... | collective-permute-start | bytes 393224 | tf_op jit(solution)/shard_map/ppermute | solution.py:27
  23.5 17.3 %copy-start.9 = (bf16[4,128,128]{2,1,0:T(8,128)(2,1)}, bf16[4,128,128]{2,1,0:T(8,128)(2,1)S(1)}, u32[]{:S(2)}) copy-start(bf16[4,128,128]{2,1,0:T(8,128)(2,1)S(1)} %collective-permute-done.1.refs_2_) | copy-start | bytes 393220
  23.5 6.2 %collective-permute-start.5 = (bf16[4,128,128]{2,1,0:T(8,128)(2,1)S(1)}, bf16[4,128,128]{2,1,0:T(8,128)(2,1)S(1)}, u32[]{:S(2)}, u32[]{:S(2)}) collective-permute-start(bf16[4,128,128]{2,1,0:T(8,128)(2,1)S(1)} %collective-permute-done.3.refs_4_), channel_id=1, source_target_pairs={{0,2},{2,0},{1,3},{3,1},{4,6},{6,4},{5,7},{7,5},{8,10},{10,8},{9,1... | collective-permute-start | bytes 393224 | tf_op jit(solution)/shard_map/ppermute | solution.py:27
  24.0 16.8 %copy-start.10 = (bf16[4,128,128]{2,1,0:T(8,128)(2,1)}, bf16[4,128,128]{2,1,0:T(8,128)(2,1)S(1)}, u32[]{:S(2)}) copy-start(bf16[4,128,128]{2,1,0:T(8,128)(2,1)S(1)} %collective-permute-done.refs_1_) | copy-start | bytes 393220
  24.0 10.8 %collective-permute-start.8 = (bf16[4,128,128]{2,1,0:T(8,128)(2,1)S(1)}, bf16[4,128,128]{2,1,0:T(8,128)(2,1)S(1)}, u32[]{:S(2)}, u32[]{:S(2)}) collective-permute-start(bf16[4,128,128]{2,1,0:T(8,128)(2,1)S(1)} %collective-permute-done.7.refs_8_.refs_12_), channel_id=1, source_target_pairs={{0,1},{1,0},{2,3},{3,2},{4,5},{5,4},{6,7},{7,6},{8,9},{9,8},{10,11... | collective-permute-start | bytes 393224 | tf_op jit(solution)/shard_map/ppermute | solution.py:27
  24.1 16.7 %copy-start.11 = (bf16[4,128,128]{2,1,0:T(8,128)(2,1)}, bf16[4,128,128]{2,1,0:T(8,128)(2,1)S(1)}, u32[]{:S(2)}) copy-start(bf16[4,128,128]{2,1,0:T(8,128)(2,1)S(1)} %collective-permute-done.15.refs_17_.refs_23_) | copy-start | bytes 393220
  24.1 15.1 %collective-permute-start.4 = (bf16[4,128,128]{2,1,0:T(8,128)(2,1)S(1)}, bf16[4,128,128]{2,1,0:T(8,128)(2,1)S(1)}, u32[]{:S(2)}, u32[]{:S(2)}) collective-permute-start(bf16[4,128,128]{2,1,0:T(8,128)(2,1)S(1)} %collective-permute-done.3.refs_4_), channel_id=1, source_target_pairs={{0,1},{1,0},{2,3},{3,2},{4,5},{5,4},{6,7},{7,6},{8,9},{9,8},{10,11... | collective-permute-start | bytes 393224 | tf_op jit(solution)/shard_map/ppermute | solution.py:27
  24.6 16.2 %copy-start.12 = (bf16[4,128,128]{2,1,0:T(8,128)(2,1)}, bf16[4,128,128]{2,1,0:T(8,128)(2,1)S(1)}, u32[]{:S(2)}) copy-start(bf16[4,128,128]{2,1,0:T(8,128)(2,1)S(1)} %collective-permute-done.13.refs_15_.refs_19_) | copy-start | bytes 393220
  24.6 16.1 %collective-permute-start.2 = (bf16[4,128,128]{2,1,0:T(8,128)(2,1)S(1)}, bf16[4,128,128]{2,1,0:T(8,128)(2,1)S(1)}, u32[]{:S(2)}, u32[]{:S(2)}) collective-permute-start(bf16[4,128,128]{2,1,0:T(8,128)(2,1)S(1)} %collective-permute-done.1.refs_2_), channel_id=1, source_target_pairs={{0,1},{1,0},{2,3},{3,2},{4,5},{5,4},{6,7},{7,6},{8,9},{9,8},{10,11... | collective-permute-start | bytes 393224 | tf_op jit(solution)/shard_map/ppermute | solution.py:27
  28.3 12.6 %copy-start.13 = (bf16[4,128,128]{2,1,0:T(8,128)(2,1)}, bf16[4,128,128]{2,1,0:T(8,128)(2,1)S(1)}, u32[]{:S(2)}) copy-start(bf16[4,128,128]{2,1,0:T(8,128)(2,1)S(1)} %collective-permute-done.9.refs_10_.refs_14_) | copy-start | bytes 393220
  28.3 12.4 %collective-permute-start.10 = (bf16[4,128,128]{2,1,0:T(8,128)(2,1)S(1)}, bf16[4,128,128]{2,1,0:T(8,128)(2,1)S(1)}, u32[]{:S(2)}, u32[]{:S(2)}) collective-permute-start(bf16[4,128,128]{2,1,0:T(8,128)(2,1)S(1)} %collective-permute-done.9.refs_10_.refs_14_), channel_id=1, source_target_pairs={{0,1},{1,0},{2,3},{3,2},{4,5},{5,4},{6,7},{7,6},{8,9},{9,8},{10,11... | collective-permute-start | bytes 393224 | tf_op jit(solution)/shard_map/ppermute | solution.py:27
  29.7 11.2 %copy-start.14 = (bf16[4,128,128]{2,1,0:T(8,128)(2,1)}, bf16[4,128,128]{2,1,0:T(8,128)(2,1)S(1)}, u32[]{:S(2)}) copy-start(bf16[4,128,128]{2,1,0:T(8,128)(2,1)S(1)} %collective-permute-done.5.refs_6_) | copy-start | bytes 393220
  29.7 11.0 %collective-permute-start.6 = (bf16[4,128,128]{2,1,0:T(8,128)(2,1)S(1)}, bf16[4,128,128]{2,1,0:T(8,128)(2,1)S(1)}, u32[]{:S(2)}, u32[]{:S(2)}) collective-permute-start(bf16[4,128,128]{2,1,0:T(8,128)(2,1)S(1)} %collective-permute-done.5.refs_6_), channel_id=1, source_target_pairs={{0,1},{1,0},{2,3},{3,2},{4,5},{5,4},{6,7},{7,6},{8,9},{9,8},{10,11... | collective-permute-start | bytes 393224 | tf_op jit(solution)/shard_map/ppermute | solution.py:27
  34.9 6.0 %copy-start.15 = (bf16[4,128,128]{2,1,0:T(8,128)(2,1)}, bf16[4,128,128]{2,1,0:T(8,128)(2,1)S(1)}, u32[]{:S(2)}) copy-start(bf16[4,128,128]{2,1,0:T(8,128)(2,1)S(1)} %collective-permute-done.8.refs_9_.refs_13_) | copy-start | bytes 393220
  34.9 14.7 %collective-permute-start.20 = (bf16[4,128,128]{2,1,0:T(8,128)(2,1)S(1)}, bf16[4,128,128]{2,1,0:T(8,128)(2,1)S(1)}, u32[]{:S(2)}, u32[]{:S(2)}) collective-permute-start(bf16[4,128,128]{2,1,0:T(8,128)(2,1)S(1)} %bitcast.12), channel_id=1, source_target_pairs={{0,8},{4,12},{8,0},{12,4},{1,9},{5,13},{9,1},{13,5},{2,10},{6,14},... | collective-permute-start | bytes 393224 | tf_op jit(solution)/shard_map/ppermute | solution.py:27
  39.2 1.7 %copy-start.16 = (bf16[4,128,128]{2,1,0:T(8,128)(2,1)}, bf16[4,128,128]{2,1,0:T(8,128)(2,1)S(1)}, u32[]{:S(2)}) copy-start(bf16[4,128,128]{2,1,0:T(8,128)(2,1)S(1)} %collective-permute-done.4.refs_5_) | copy-start | bytes 393220
  39.2 10.9 %collective-permute-start.18 = (bf16[4,128,128]{2,1,0:T(8,128)(2,1)S(1)}, bf16[4,128,128]{2,1,0:T(8,128)(2,1)S(1)}, u32[]{:S(2)}, u32[]{:S(2)}) collective-permute-start(bf16[4,128,128]{2,1,0:T(8,128)(2,1)S(1)} %collective-permute-done.16.refs_8_), channel_id=1, source_target_pairs={{0,2},{2,0},{1,3},{3,1},{4,6},{6,4},{5,7},{7,5},{8,10},{10,8},{9,1... | collective-permute-start | bytes 393224 | tf_op jit(solution)/shard_map/ppermute | solution.py:27
  40.7 0.7 copy-start.17
  40.7 0.7 copy-start.18
  40.7 0.7 copy-start.19
  49.0 8.4 %collective-permute-start.22 = (f32[128,512]{1,0:T(8,128)}, f32[128,512]{1,0:T(8,128)S(1)}, u32[]{:S(2)}, u32[]{:S(2)}) collective-permute-start(f32[128,512]{1,0:T(8,128)} %get-tuple-element.14), channel_id=1, source_target_pairs={{0,2},{2,0},{1,3},{3,1},{4,6},{6,4},{5,7},{7,5},{8,10},{10,8},{9,1... | collective-permute-start | bytes 786440 | tf_op jit(solution)/shard_map/ppermute | solution.py:27
  49.6 1.5 %collective-permute-start.17 = (bf16[4,128,128]{2,1,0:T(8,128)(2,1)S(1)}, bf16[4,128,128]{2,1,0:T(8,128)(2,1)S(1)}, u32[]{:S(2)}, u32[]{:S(2)}) collective-permute-start(bf16[4,128,128]{2,1,0:T(8,128)(2,1)S(1)} %collective-permute-done.16.refs_8_), channel_id=1, source_target_pairs={{0,1},{1,0},{2,3},{3,2},{4,5},{5,4},{6,7},{7,6},{8,9},{9,8},{10,11... | collective-permute-start | bytes 393224 | tf_op jit(solution)/shard_map/ppermute | solution.py:27
  49.6 7.8 %copy-start.20 = (bf16[4,128,128]{2,1,0:T(8,128)(2,1)}, bf16[4,128,128]{2,1,0:T(8,128)(2,1)S(1)}, u32[]{:S(2)}) copy-start(bf16[4,128,128]{2,1,0:T(8,128)(2,1)S(1)} %collective-permute-done.20.refs_20_) | copy-start | bytes 393220
  49.6 1.5 %collective-permute-start.21 = (bf16[4,128,128]{2,1,0:T(8,128)(2,1)S(1)}, bf16[4,128,128]{2,1,0:T(8,128)(2,1)S(1)}, u32[]{:S(2)}, u32[]{:S(2)}) collective-permute-start(bf16[4,128,128]{2,1,0:T(8,128)(2,1)S(1)} %collective-permute-done.20.refs_20_), channel_id=1, source_target_pairs={{0,1},{1,0},{2,3},{3,2},{4,5},{5,4},{6,7},{7,6},{8,9},{9,8},{10,11... | collective-permute-start | bytes 393224 | tf_op jit(solution)/shard_map/ppermute | solution.py:27
  50.1 7.3 %copy-start.21 = (bf16[4,128,128]{2,1,0:T(8,128)(2,1)}, bf16[4,128,128]{2,1,0:T(8,128)(2,1)S(1)}, u32[]{:S(2)}) copy-start(bf16[4,128,128]{2,1,0:T(8,128)(2,1)S(1)} %collective-permute-done.18.refs_10_) | copy-start | bytes 393220
  50.1 1.3 %collective-permute-start.19 = (bf16[4,128,128]{2,1,0:T(8,128)(2,1)S(1)}, bf16[4,128,128]{2,1,0:T(8,128)(2,1)S(1)}, u32[]{:S(2)}, u32[]{:S(2)}) collective-permute-start(bf16[4,128,128]{2,1,0:T(8,128)(2,1)S(1)} %collective-permute-done.18.refs_10_), channel_id=1, source_target_pairs={{0,1},{1,0},{2,3},{3,2},{4,5},{5,4},{6,7},{7,6},{8,9},{9,8},{10,11... | collective-permute-start | bytes 393224 | tf_op jit(solution)/shard_map/ppermute | solution.py:27
  51.1 6.3 %copy-start.23 = (bf16[4,128,128]{2,1,0:T(8,128)(2,1)}, bf16[4,128,128]{2,1,0:T(8,128)(2,1)S(1)}, u32[]{:S(2)}) copy-start(bf16[4,128,128]{2,1,0:T(8,128)(2,1)S(1)} %collective-permute-done.21.refs_21_) | copy-start | bytes 393220
  51.1 6.3 %copy-start.22 = (bf16[4,128,128]{2,1,0:T(8,128)(2,1)}, bf16[4,128,128]{2,1,0:T(8,128)(2,1)S(1)}, u32[]{:S(2)}) copy-start(bf16[4,128,128]{2,1,0:T(8,128)(2,1)S(1)} %collective-permute-done.17.refs_9_) | copy-start | bytes 393220
  51.4 6.0 %copy-start.24 = (bf16[4,128,128]{2,1,0:T(8,128)(2,1)}, bf16[4,128,128]{2,1,0:T(8,128)(2,1)S(1)}, u32[]{:S(2)}) copy-start(bf16[4,128,128]{2,1,0:T(8,128)(2,1)S(1)} %collective-permute-done.19.refs_11_) | copy-start | bytes 393220
  57.4 0.7 copy-start.2

commit v2 on v0

v2 whole, which is shorter than its diff:
```python
import functools
import math

import jax
import jax.numpy as jnp
from jax import lax
from jax.experimental import pallas as pl
from jax.experimental.pallas import tpu as pltpu
from jax.sharding import PartitionSpec as P

ZS = 4
BF = jnp.bfloat16
F32 = jnp.float32
VMEM = pl.BlockSpec(memory_space=pltpu.VMEM)
SMEM = pl.BlockSpec(memory_space=pltpu.SMEM)
HBM = pl.BlockSpec(memory_space=pltpu.HBM)
MIB = 2**20
TINY = pl.CostEstimate(flops=1000, bytes_accessed=1000, transcendentals=0)


def params(mib):
    return pltpu.CompilerParams(vmem_limit_bytes=mib * MIB)


def shape(dims, dtype):
    return jax.ShapeDtypeStruct(dims, dtype)


def swap(x, axis, k):
    return lax.ppermute(x, axis, [(i, i ^ k) for i in range(lax.axis_size(axis))])


def rotate(x, axis, k):
    n = lax.axis_size(axis)
    if k % n == 0:
        return x
    return lax.ppermute(x, axis, [(i, (i + k) % n) for i in range(n)])


def after(*values):
    return lax.optimization_barrier(values)


def y_inside(lanes, dy, sub, count):
    lane = lax.broadcasted_iota(jnp.int32, (16, lanes), 1)
    pos = lane + sub * (lanes // count)
    pos = jnp.where(pos >= lanes, pos - lanes, pos) + ZS * dy
    return jnp.where((pos >= 0) & (pos < lanes), 1.0, 0.0).astype(BF)


def z_inside(lanes, dz, dtype):
    z = (lax.broadcasted_iota(jnp.int32, (16, lanes), 1) & (ZS - 1)) + dz
    return jnp.where((z >= 0) & (z < ZS), 1.0, 0.0).astype(dtype)


def moved(v, step, mask):
    if step == 0:
        return v
    lanes = v.shape[-1]
    turned = pltpu.roll(v, (-step) % lanes, v.ndim - 1)
    return turned * mask[:1]


def pack_kernel(act_ref, grad_ref, a_ref, g_ref, both_ref):
    planes = act_ref.shape[1]
    for x in range(planes):
        a = act_ref[:, x, :]
        g = grad_ref[:, x, :]
        a_ref[x] = a
        g_ref[x] = g
        both_ref[x] = a
        both_ref[planes + x] = g


def pack(activations, out_grad):
    local, planes, span = activations.shape
    one = shape((planes, local, span), BF)
    return pl.pallas_call(
        pack_kernel,
        out_shape=(one, one, shape((2 * planes, local, span), BF)),
        in_specs=[VMEM] * 2,
        out_specs=(VMEM,) * 3,
        compiler_params=params(8),
        cost_estimate=TINY,
    )(activations, out_grad)


def halves_kernel(count, *refs):
    for n in range(count):
        rows = refs[n].shape[0] // 2
        for half in range(2):
            refs[count + 2 * n + half][...] = refs[n][half * rows : (half + 1) * rows]


def halves(*arrays):
    outs = []
    for a in arrays:
        outs += [shape((a.shape[0] // 2,) + a.shape[1:], BF)] * 2
    return pl.pallas_call(
        functools.partial(halves_kernel, len(arrays)),
        out_shape=outs,
        in_specs=[VMEM] * len(arrays),
        out_specs=[VMEM] * len(outs),
        compiler_params=params(8),
        cost_estimate=TINY,
    )(*arrays)


def list_of(blocks):
    return {name: n for n, name in enumerate(blocks)}


def filter_kernel(n_chan, ids, w_ref, wt_ref, wn_ref, rows):
    local, columns = w_ref.shape
    total = columns // 27
    mine = ids[1]
    for at in range(0, columns, 128):
        rows[at : at + 128, :] = w_ref[:, at : at + 128].astype(F32).T
    for t in range(27):
        ab, c = t // 3, t % 3
        for j in range(n_chan):
            true = lax.rem(mine + j, n_chan)
            v = rows[pl.ds(true * (local * 27) + t, local, stride=27), :]
            row = (j * 3 + c) * local
            wt_ref[row : row + local, ab * local : (ab + 1) * local] = v.astype(BF)
            at = ab * total + j * local
            wn_ref[c * local : (c + 1) * local, at : at + local] = v.T.astype(BF)


def arrange_filter(ids, weight, n_chan):
    local, columns = weight.shape
    total = columns // 27
    return pl.pallas_call(
        functools.partial(filter_kernel, n_chan),
        out_shape=(shape((3 * total, 9 * local), BF), shape((3 * local, 9 * total), BF)),
        in_specs=[SMEM, VMEM],
        out_specs=(VMEM, VMEM),
        scratch_shapes=[pltpu.VMEM((columns, local), F32)],
        compiler_params=params(16),
        cost_estimate=TINY,
    )(ids, weight)


def z_taps(v, rows, cells, direction):
    out = v[rows : 2 * rows]
    for c in (0, 2):
        dz = direction * (c - 1)
        mask = z_inside(cells, dz, F32)
        out = out + moved(v[c * rows : (c + 1) * rows], dz, mask)
    return out


def edge_planes(refs, layout, sizes, near, tile):
    n_tile, _, n_sub = sizes

    def row(key, slot, x):
        return jnp.concatenate([refs[layout[key + (slot, u)]][x] for u in range(n_sub)], axis=1)

    def plane(key, x, planes):
        if 0 < x <= planes:
            return row(key, 0, x - 1)
        beyond = x > planes
        even, odd = near[beyond]
        at = 0 if beyond else planes - 1
        v = row(key, even, at)
        if odd != even:
            v = jnp.where((tile & 1) == 1, row(key, odd, at), v)
        inside = tile < n_tile - 1 if beyond else tile > 0
        return jnp.where(inside, v, jnp.zeros((), BF))

    return plane


def conv_kernel(sizes, layout, near, ids, *refs):
    *arrays, wn_ref, conv_ref, act_cols = refs
    _, n_chan, n_sub = sizes
    local, planes, span = conv_ref.shape
    total = n_chan * local
    cells = planes * span
    plane = edge_planes(arrays, layout, sizes, near, ids[0])
    masks = [y_inside(span * n_sub, dy, ids[2], n_sub) for dy in (-1, 0, 1)]
    for x in range(planes + 2):
        for j in range(n_chan):
            v = plane(("act", j), x, planes)
            for b in range(3):
                s = moved(v, ZS * (b - 1), masks[b])
                at = b * total + j * local
                act_cols[at : at + local, x * span : (x + 1) * span] = s[:, :span]
    out = jnp.zeros((3 * local, cells), F32)
    for a in range(3):
        out += jnp.dot(
            wn_ref[:, a * 3 * total : (a + 1) * 3 * total],
            act_cols[:, a * span : a * span + cells],
            preferred_element_type=F32,
        )
    out = z_taps(out, local, cells, 1)
    for x in range(planes):
        conv_ref[:, x, :] = out[:, x * span : (x + 1) * span].astype(BF)


def convolve(ids, blocks, wn, near, sizes, block):
    local, planes, span = block
    arrays = list(blocks.values())
    return pl.pallas_call(
        functools.partial(conv_kernel, sizes, list_of(blocks), near),
        out_shape=shape(block, BF),
        in_specs=[SMEM] + [VMEM] * (len(arrays) + 1),
        out_specs=VMEM,
        scratch_shapes=[pltpu.VMEM((3 * sizes[1] * local, (planes + 2) * span), BF)],
        compiler_params=params(16),
        cost_estimate=TINY,
    )(ids, *arrays, wn)


def terms_kernel(sizes, layout, near, ids, *refs):
    _, n_chan, n_sub = sizes
    arrays, wt_ref = refs[: -2 - n_chan], refs[-2 - n_chan]
    part_refs, grad_cols = refs[-1 - n_chan : -1], refs[-1]
    _, local, span = arrays[0].shape
    cells = part_refs[0].shape[1]
    planes = cells // span
    plane = edge_planes(arrays, layout, sizes, near, ids[0])
    masks = [y_inside(span * n_sub, dy, ids[2], n_sub) for dy in (-1, 0, 1)]
    for x in range(planes + 2):
        v = plane(("grad",), x, planes)
        for b in range(3):
            s = moved(v, ZS * (1 - b), masks[2 - b])
            grad_cols[b * local : (b + 1) * local, x * span : (x + 1) * span] = s[:, :span]
    for j in reversed(range(n_chan)):
        part = jnp.zeros((3 * local, cells), F32)
        for a in range(3):
            part += jnp.dot(
                wt_ref[j * 3 * local : (j + 1) * 3 * local, a * 3 * local : (a + 1) * 3 * local],
                grad_cols[:, (2 - a) * span : (2 - a) * span + cells],
                preferred_element_type=F32,
            )
        part_refs[j][...] = z_taps(part, local, cells, -1)


def input_terms(ids, blocks, wt, near, sizes, block):
    local, planes, span = block
    n_chan = sizes[1]
    arrays = list(blocks.values())
    return pl.pallas_call(
        functools.partial(terms_kernel, sizes, list_of(blocks), near),
        out_shape=[shape((local, planes * span), F32)] * n_chan,
        in_specs=[SMEM] + [VMEM] * (len(arrays) + 1),
        out_specs=[VMEM] * n_chan,
        scratch_shapes=[pltpu.VMEM((3 * local, (planes + 2) * span), BF)],
        compiler_params=params(16),
        cost_estimate=TINY,
    )(ids, *arrays, wt)


def update_kernel(sizes, block, layout, count, runs, earlier, final, scale, ids, *refs):
    n_tile, n_chan, n_sub = sizes
    local, planes, span = block
    wide = span * n_sub
    total = n_chan * local
    refs = list(refs)
    arrays = [refs.pop(0) for _ in range(count)]
    edges = [(refs.pop(0), refs.pop(0)) for _ in earlier]
    acc_in = refs.pop(0) if earlier else None
    parts = [refs.pop(0) for _ in range(n_chan)] if final else []
    outs = [refs.pop(0) for _ in range(2 if final else 2 * len(runs) + 1)]
    windows = [(refs.pop(0), refs.pop(0)) for _ in runs]
    rows, out_vmem, sems = refs if final else (None,) * 3
    mine, sub = ids[1], ids[2]
    ymask = [y_inside(wide, dy, sub, n_sub) for dy in (-1, 0, 1)]
    zmask = [z_inside(wide, dz, BF) for dz in (-1, 0, 1)]

    def row(key, slot, x):
        return jnp.concatenate([arrays[layout[key + (slot, u)]][x] for u in range(n_sub)], axis=1)

    known = []
    for (act_edge, grad_edge), (place, length) in zip(edges, earlier, strict=True):
        ends = [(lambda n=n, e=e: e[n]) for e in (act_edge, grad_edge) for n in range(2)]
        known.append((ids[3 + place], length, ends))
    spans = []
    for (act_win, grad_win), slots in zip(windows, runs, strict=True):
        start = ids[3 + slots[0][1]]
        long = len(slots) * planes
        for place, _, slot in slots:
            for x in range(planes):
                at = (x + 1) * wide
                if len(slots) > 1:
                    at = pl.multiple_of((ids[3 + place] - start) * (planes * wide) + at, wide)
                for j in range(n_chan):
                    v = row(("act", j), slot, x)
                    for b in range(3):
                        top = b * total + j * local
                        act_win[top : top + local, pl.ds(at, wide)] = moved(
                            v, ZS * (b - 1), ymask[b]
                        )
                v = row(("grad",), slot, x)
                for c in range(3):
                    grad_win[c * local : (c + 1) * local, pl.ds(at, wide)] = moved(
                        v, 1 - c, zmask[2 - c]
                    )
        if known:
            low, high = slice(0, wide), slice((long + 1) * wide, (long + 2) * wide)
            for win in (act_win, grad_win):
                for side in (low, high):
                    win[:, side] = jnp.zeros((win.shape[0], wide), BF)
            for begin, length, ends in known:

                @pl.when(begin + length == start)
                def _():
                    act_win[:, low] = ends[1]()
                    grad_win[:, low] = ends[3]()

                @pl.when(begin == start + len(slots))
                def _():
                    act_win[:, high] = ends[0]()
                    grad_win[:, high] = ends[2]()

        if known:
            spans.append([(1, long + 1), (1, long), (0, long)])
        else:
            spans.append([(2, long), (1, long), (1, long - 1)])
        sides = [slice(wide, 2 * wide), slice(long * wide, (long + 1) * wide)]
        ends = [(lambda w=w, s=s: w[:, s]) for w in (act_win, grad_win) for s in sides]
        known.append((start, len(slots), ends))
        if not final:
            n = 2 * (len(spans) - 1)
            for side in range(2):
                outs[n][side] = ends[side]()
                outs[n + 1][side] = ends[2 + side]()

    if final:
        out_ref, ig_ref = outs
        ig = parts[0][...]
        for j in range(1, n_chan):
            ig = ig + parts[j][...]
        for x in range(planes):
            ig_ref[:, x, :] = ig[:, x * span : (x + 1) * span].astype(BF)

    for a in range(3):
        for b in range(3):
            r = acc_in[a * 3 + b] if earlier else None
            for (act_win, grad_win), ranges in zip(windows, spans, strict=True):
                first, last = ranges[a]
                d = lax.dot_general(
                    grad_win[:, first * wide : (last + 1) * wide],
                    act_win[
                        b * total : (b + 1) * total, (first + a - 1) * wide : (last + a) * wide
                    ],
                    (((1,), (1,)), ((), ())),
                    preferred_element_type=F32,
                )
                r = d if r is None else r + d
            if not final:
                outs[-1][a * 3 + b] = r
                continue
            for c in range(3):
                for j in range(n_chan):
                    true = lax.rem(mine + j, n_chan)
                    at = true * (local * 27) + a * 9 + b * 3 + c
                    tap = r[c * local : (c + 1) * local, j * local : (j + 1) * local]
                    rows[pl.ds(at, local, stride=27), :] = tap.T
    if final:
        copies = []
        width = total * 27 // sems.shape[0]
        for n in range(sems.shape[0]):
            for at in range(n * width, (n + 1) * width, 128):
                out_vmem[:, at : at + 128] = rows[at : at + 128, :].T * scale
            some = slice(n * width, (n + 1) * width)
            copies.append(pltpu.make_async_copy(out_vmem.at[:, some], out_ref.at[:, some], sems.at[n]))
            copies[-1].start()
        for copy in copies:
            copy.wait()


def update(ids, blocks, runs, earlier, carried, parts, scale, sizes, block):
    n_tile, n_chan, n_sub = sizes
    local, planes, span = block
    wide = span * n_sub
    total = n_chan * local
    final = parts is not None
    arrays = list(blocks.values())
    extra = list(carried) + list(parts or [])
    if final:
        outs = [shape((local, total * 27), F32), shape(block, BF)]
    else:
        outs = [shape((2, 3 * n, wide), BF) for _ in runs for n in (total, local)]
        outs.append(shape((9, 3 * local, total), F32))
    scratch = [
        pltpu.VMEM((3 * n, (len(slots) * planes + 2) * wide), BF)
        for slots in runs
        for n in (total, local)
    ]
    if final:
        scratch.append(pltpu.VMEM((total * 27, local), F32))
        scratch.append(pltpu.VMEM((local, total * 27), F32))
        scratch.append(pltpu.SemaphoreType.DMA((3,)))
    return pl.pallas_call(
        functools.partial(
            update_kernel,
            sizes,
            block,
            list_of(blocks),
            len(arrays),
            runs,
            earlier,
            final,
            scale,
        ),
        out_shape=outs,
        in_specs=[SMEM] + [VMEM] * (len(arrays) + len(extra)),
        out_specs=[HBM, VMEM] if final else [VMEM] * len(outs),
        scratch_shapes=scratch,
        compiler_params=params(28 if n_tile == 4 else 58),
        cost_estimate=TINY,
    )(ids, *arrays, *extra)


def body(activations, out_grad, weight):
    block = local, planes, span = activations.shape
    sizes = n_tile, n_chan, n_sub = tuple(lax.axis_size(a) for a in ("tile", "chan", "sub"))
    scale = 1.0 / math.sqrt(planes * span * n_tile * n_sub)
    tile, chan, sub = (lax.axis_index(a) for a in ("tile", "chan", "sub"))
    paired = n_tile == 4
    if paired:
        places = [tile, tile ^ 1, tile ^ 2, tile ^ 3, tile & 2]
    else:
        places = [lax.rem(tile - k + n_tile, n_tile) for k in range(n_tile)] + [0 * tile]
    ids = jnp.stack([tile, chan, sub] + places).astype(jnp.int32)
    chans, subs = range(n_chan), range(n_sub)

    act, grad, both = pack(activations, out_grad)
    blocks = {}

    def share(v, *name):
        for u in subs:
            blocks[name + (u,)] = rotate(v, "sub", -u)

    def only(slots, kind=None):
        return {k: v for k, v in blocks.items() if k[-2] in slots and kind in (None, k[0])}

    def add(runs, earlier, carried, parts=None):
        used = only({slot for slots in runs for _, _, slot in slots})
        return update(ids, used, runs, earlier, carried, parts, scale, sizes, block)

    if not paired:
        wt, wn = arrange_filter(ids, weight, n_chan)
        for k in range(n_tile):
            a, g = rotate(act, "tile", k), rotate(grad, "tile", k)
            share(g, "grad", k)
            for j in chans:
                share(rotate(a, "chan", -j), "act", j, k)
        near = ((1, 1), (n_tile - 1, n_tile - 1))
        close = {0, 1, n_tile - 1}
        conv_out = convolve(ids, only(close, "act"), wn, near, sizes, block)
        parts = input_terms(ids, only(close, "grad"), wt, near, sizes, block)
        parts = [rotate(part, "chan", j) for j, part in enumerate(parts)]
        runs = (tuple((k, n_tile, k) for k in range(n_tile)),)
        weight_grad, input_grad = add(runs, (), (), parts)
        return conv_out, input_grad, weight_grad

    near = ((3, 1), (1, 3))
    first = swap(both, "tile", 1)
    third = swap(both, "tile", 3)
    wt, wn = arrange_filter(ids, weight, n_chan)
    for j in chans:
        share(rotate(act, "chan", -j), "act", j, 0)
    share(grad, "grad", 0)
    act_0, grad_0, acc = add((((0, 0, 0),),), (), ())
    first, third, wt, wn, acc = after(first, third, wt, wn, acc)
    far = swap(after(both, third)[0], "tile", 2)
    act_1, grad_1, act_3, grad_3 = halves(first, third)
    beside = [rotate(v, "chan", -j) for j in chans[1:] for v in (act_1, act_3)]
    share(grad_1, "grad", 1)
    share(grad_3, "grad", 3)
    share(act_1, "act", 0, 1)
    share(act_3, "act", 0, 3)
    parts = input_terms(ids, only({0, 1, 3}, "grad"), wt, near, sizes, block)
    tail = after(*beside, *parts)
    beside, parts = tail[: len(beside)], tail[len(beside) :]
    parts = [rotate(part, "chan", j) for j, part in enumerate(parts)]
    for n, v in enumerate(beside):
        share(v, "act", 1 + n // 2, (1, 3)[n % 2])
    runs = (((1, 1, 1),), ((3, 3, 3),))
    *edges, acc = add(runs, ((0, 1),), (act_0, grad_0, acc))
    far, acc, wn, *parts = after(far, acc, wn, *parts)
    act_2, grad_2 = halves(far)
    beside = [rotate(act_2, "chan", -j) for j in chans[1:]]
    conv_out = convolve(ids, only({0, 1, 3}, "act"), wn, near, sizes, block)
    conv_out, act_2, grad_2, *beside = after(conv_out, act_2, grad_2, *beside)
    share(act_2, "act", 0, 2)
    share(grad_2, "grad", 2)
    for j, v in enumerate(beside, 1):
        share(v, "act", j, 2)
    runs, earlier = (((2, 2, 2),),), ((0, 1), (1, 1), (3, 1))
    weight_grad, input_grad = add(runs, earlier, (act_0, grad_0, *edges, acc), parts)
    return conv_out, input_grad, weight_grad


def solution(mesh):
    placed = (
        P("chan", ("groups", "tile"), "sub"),
        P("chan", ("groups", "tile"), "sub"),
        P("chan", None),
    )
    return jax.shard_map(
        body,
        mesh=mesh,
        in_specs=placed,
        out_specs=(
            P("chan", ("groups", "tile"), "sub"),
            P("chan", ("groups", "tile"), "sub"),
            P(("groups", "chan"), None),
        ),
        check_vma=False,
    )
```

time: 234 us -> 54.5 us (0.23)
  local copies, waits for them, and re-layouts: 71.7 us -> 3.36 us
  waiting for transfers between devices: 71.2 us -> 12.6 us
  matrix products: 37.1 us -> 0 us
  Pallas kernels: 0 us -> 24 us
  between operations: 17.2 us -> 0.88 us
  starting transfers between devices: 21.6 us -> 13.4 us
  other arithmetic: 7.03 us -> 0 us
  blocking collectives: 6.68 us -> 0 us
    psum x1 -> x0, waiting for transfers between devices: 71.2 us -> none  [body(): weight_grad = lax.psum(local_grad, ('tile', 'sub'))]
    slice x33 -> x0, local copies, waits for them, and re-layouts: 47.5 us -> none  [the longest x29 41.3 us: body(): columns = by_tap[tap_idx]]
    dot_general x81 -> x0, matrix products: 37.1 us -> none  [the longest x27 16 us: body(): jnp.dot(columns, window, preferred_element_type=jnp.float32)]
    pallas_call x0 -> x9, Pallas kernels: none -> 24 us  [the longest x3 16.1 us: update(): pl.pallas_call(functools.partial(update_kernel, sizes, block, list_of(blo...]
    ppermute x8 -> x20, waiting for transfers between devices: 0.02 us -> 12.6 us  [the longest x17 7.26 us: rotate(): return lax.ppermute(x, axis, [(i, (i + k) % n) for i in range(n)])]
    unnamed x150 -> x6, local copies, waits for them, and re-layouts: 12.9 us -> 3.28 us
    mul x2 -> x0, local copies, waits for them, and re-layouts: 8.77 us -> none  [body(): grad_acc.transpose(1, 2, 0).reshape(local_ch, total_ch * 27) * scale]
    ppermute x8 -> x20, starting transfers between devices: 21.3 us -> 13.4 us  [the longest x17 9.17 us: rotate(): return lax.ppermute(x, axis, [(i, (i + k) % n) for i in range(n)])]
  transfers between devices with their start and end apart: 10 -> 20, of which waited for: 1 -> 12; matrix products, arithmetic and copies ran while one was open for 44% -> 0% of each run, Pallas kernels for 0% -> 29%
where the time goes in v2:
time: 54.5 us; the launch traced here: 54.3 us
  Pallas kernels  24 us (44%)
  starting transfers between devices  13.4 us (25%)
  waiting for transfers between devices  12.6 us (23%)
  local copies, waits for them, and re-layouts  3.36 us (6%)
  between operations  0.88 us (2%)
    pallas_call x3, Pallas kernels, update(): pl.pallas_call(functools.partial(update_kernel, sizes, block, list_of(blo...  16.1 us
    ppermute x17, starting transfers between devices, rotate(): return lax.ppermute(x, axis, [(i, (i + k) % n) for i in range(n)])  9.17 us
    ppermute x17, waiting for transfers between devices, rotate(): return lax.ppermute(x, axis, [(i, (i + k) % n) for i in range(n)])  7.26 us
    ppermute x3, waiting for transfers between devices, swap(): lax.ppermute(x, axis, [(i, i ^ k) for i in range(lax.axis_size(axis))])  5.34 us
    ppermute x3, starting transfers between devices, swap(): lax.ppermute(x, axis, [(i, i ^ k) for i in range(lax.axis_size(axis))])  4.24 us
    unnamed x6, local copies, waits for them, and re-layouts  3.28 us
    pallas_call x1, Pallas kernels, convolve(): pl.pallas_call(functools.partial(conv_kernel, sizes, list_of(blocks), nea...  2.95 us
    pallas_call x1, Pallas kernels, input_terms(): pl.pallas_call(functools.partial(terms_kernel, sizes, list_of(blocks), ne...  2.2 us
  transfers between devices with their start and end apart: 20, of which 12 were waited for; matrix products, arithmetic and copies ran while one was open for 0% of the time, Pallas kernels for 29%

profile of v2, /device:TPU:0, one launch (start us, length us, event | category | flops | bytes accessed | tf_op | source)
XLA Modules:
  0.0 54.3 jit_solution(3511962919073868471)
XLA Ops:
  0.6 0.0 copy-start.1
  0.6 0.9 %copy-done.1 = bf16[128,4,128]{2,1,0:T(4,128)(2,1)S(1)} copy-done((bf16[128,4,128]{2,1,0:T(4,128)(2,1)S(1)}, bf16[128,4,128]{2,1,0:T(4,128)(2,1)}, u32[]{:S(2)}) %copy-start.1) | copy-done | bytes 131096
  1.5 0.0 copy-start.2
  1.5 0.9 %copy-done.2 = bf16[128,4,128]{2,1,0:T(4,128)(2,1)S(1)} copy-done((bf16[128,4,128]{2,1,0:T(4,128)(2,1)S(1)}, bf16[128,4,128]{2,1,0:T(4,128)(2,1)}, u32[]{:S(2)}) %copy-start.2) | copy-done | bytes 131096
  2.4 0.7 %shard_map.58 = (bf16[4,128,128]{2,1,0:T(8,128)(2,1)S(1)}, bf16[4,128,128]{2,1,0:T(8,128)(2,1)S(1)}, bf16[8,128,128]{2,1,0:T(8,128)(2,1)S(1)}) custom-call(bf16[128,4,128]{2,1,0:T(4,128)(2,1)S(1)} %copy-done.1, bf16[128,4,128]{2,1,0:T(4,128)(2,1)S(1)} %copy-done.2), custom_call_target="tpu_custom_call" | custom-call | flops 1000 | bytes 1000 | tf_op jit(solution)/shard_map/pallas_call | solution.py:78
  3.1 3.0 %collective-permute-start.1 = (bf16[4,128,128]{2,1,0:T(8,128)(2,1)S(1)}, bf16[4,128,128]{2,1,0:T(8,128)(2,1)S(1)}, u32[]{:S(2)}, u32[]{:S(2)}) collective-permute-start(bf16[4,128,128]{2,1,0:T(8,128)(2,1)S(1)} %get-tuple-element.45.refs_0_), channel_id=1, source_target_pairs={{0,2},{2,0},{1,3},{3,1},{4,6},{6,4},{5,7},{7,5},{8,10},{10,8},{9,1... | collective-permute-start | bytes 393224 | tf_op jit(solution)/shard_map/ppermute | solution.py:37
  6.1 3.6 %collective-permute-start.4 = (bf16[8,128,128]{2,1,0:T(8,128)(2,1)S(1)}, bf16[8,128,128]{2,1,0:T(8,128)(2,1)S(1)}, u32[]{:S(2)}, u32[]{:S(2)}) collective-permute-start(bf16[8,128,128]{2,1,0:T(8,128)(2,1)S(1)} %get-tuple-element.62), channel_id=1, source_target_pairs={{0,12},{4,8},{8,4},{12,0},{1,13},{5,9},{9,5},{13,1},{2,14},{6,10},... | collective-permute-start | bytes 786440 | tf_op jit(solution)/shard_map/ppermute | solution.py:30
  9.7 0.0 collective-permute-start.3
  9.7 0.0 collective-permute-start
  9.7 0.5 collective-permute-start.5
  10.2 0.0 collective-permute-done.1.refs_2_
  10.2 0.0 collective-permute-start.2
  10.2 0.1 stack.32.ids
  10.3 0.0 copy-start
  10.3 1.5 %copy-done = bf16[128,6912]{1,0:T(8,128)(2,1)S(1)} copy-done((bf16[128,6912]{1,0:T(8,128)(2,1)S(1)}, bf16[128,6912]{1,0:T(8,128)(2,1)}, u32[]{:S(2)}) %copy-start) | copy-done | bytes 1769496
  11.8 2.0 %shard_map.59 = (bf16[768,1152]{1,0:T(8,128)(2,1)S(1)}, bf16[384,2304]{1,0:T(8,128)(2,1)S(1)}) custom-call(s32[8]{0:T(128)S(1)} %stack.32.ids, bf16[128,6912]{1,0:T(8,128)(2,1)S(1)} %copy-done), custom_call_target="tpu_custom_call" | custom-call | flops 1000 | bytes 1000 | tf_op jit(solution)/shard_map/pallas_call | solution.py:133
  13.8 0.0 collective-permute-done.5.refs_5_.refs_1_
  13.9 0.0 collective-permute-done.refs_1_
  13.9 0.0 collective-permute-done.2.refs_3_
  13.9 2.3 %shard_map.60 = (bf16[2,768,256]{2,1,0:T(8,128)(2,1)S(1)}, bf16[2,384,256]{2,1,0:T(8,128)(2,1)S(1)}, f32[9,384,256]{2,1,0:T(8,128)S(1)}) custom-call(s32[8]{0:T(128)S(1)} %stack.32.ids, bf16[4,128,128]{2,1,0:T(8,128)(2,1)S(1)} %get-tuple-element.45.refs_0_, bf16[4,128,128]{2,1,0:T(8,128)(2,1)S(1)} %collective-permute-done.refs_1_, ...), custom_call_target="tpu_custom_call" | custom-call | flops 1000 | bytes 1000 | tf_op jit(solution)/shard_map/pallas_call | solution.py:396
  16.2 1.0 %collective-permute-done.4.refs_1_ = bf16[8,128,128]{2,1,0:T(8,128)(2,1)S(1)} collective-permute-done((bf16[8,128,128]{2,1,0:T(8,128)(2,1)S(1)}, bf16[8,128,128]{2,1,0:T(8,128)(2,1)S(1)}, u32[]{:S(2)}, u32[]{:S(2)}) %collective-permute-start.4) | collective-permute-done | bytes 262176 | tf_op jit(solution)/shard_map/ppermute | solution.py:30
  17.2 4.3 %collective-permute-done.3.refs_0_ = bf16[8,128,128]{2,1,0:T(8,128)(2,1)S(1)} collective-permute-done((bf16[8,128,128]{2,1,0:T(8,128)(2,1)S(1)}, bf16[8,128,128]{2,1,0:T(8,128)(2,1)S(1)}, u32[]{:S(2)}, u32[]{:S(2)}) %collective-permute-start.3) | collective-permute-done | bytes 262176 | tf_op jit(solution)/shard_map/ppermute | solution.py:30
  21.5 0.1 collective-permute-start.10
  21.6 0.5 collective-permute-start.11
  22.1 0.5 collective-permute-start.8
  22.6 1.5 %collective-permute-start.9 = (bf16[4,128,128]{2,1,0:T(8,128)(2,1)S(1)}, bf16[4,128,128]{2,1,0:T(8,128)(2,1)S(1)}, u32[]{:S(2)}, u32[]{:S(2)}) collective-permute-start(bf16[4,128,128]{2,1,0:T(8,128)(2,1)S(1)} %get-tuple-element.54.refs_6_), channel_id=1, source_target_pairs={{0,2},{2,0},{1,3},{3,1},{4,6},{6,4},{5,7},{7,5},{8,10},{10,8},{9,1... | collective-permute-start | bytes 393224 | tf_op jit(solution)/shard_map/ppermute | solution.py:37
  24.1 0.0 collective-permute-start.6
  24.1 0.0 collective-permute-done.10.refs_3_.refs_1_
  24.1 0.6 %collective-permute-start.14 = (bf16[8,128,128]{2,1,0:T(8,128)(2,1)S(1)}, bf16[8,128,128]{2,1,0:T(8,128)(2,1)S(1)}, u32[]{:S(2)}, u32[]{:S(2)}) collective-permute-start(bf16[8,128,128]{2,1,0:T(8,128)(2,1)S(1)} %get-tuple-element.62), channel_id=1, source_target_pairs={{0,8},{4,12},{8,0},{12,4},{1,9},{5,13},{9,1},{13,5},{2,10},{6,14},... | collective-permute-start | bytes 786440 | tf_op jit(solution)/shard_map/ppermute | solution.py:30
  24.8 0.0 collective-permute-done.11.refs_5_.refs_3_
  24.8 2.2 %shard_map.62 = (f32[128,512]{1,0:T(8,128)S(1)}, f32[128,512]{1,0:T(8,128)S(1)}) custom-call(s32[8]{0:T(128)S(1)} %stack.32.ids, bf16[4,128,128]{2,1,0:T(8,128)(2,1)S(1)} %get-tuple-element.49.refs_4_.refs_0_, bf16[4,128,128]{2,1,0:T(8,128)(2,1)S(1)} %collective-permute-done.5.refs_5_.refs_1_, bf16[4,128,128]{2,1,0:T(8,128)(2,1)S(1)} %get-tuple-element.55.refs_2_.refs_0_, ...), custom_call_target="tpu_custom_call" | custom-call | flops 1000 | bytes 1000 | tf_op jit(solution)/shard_map/pallas_call | solution.py:244
  27.0 1.5 %collective-permute-done.8.refs_8_ = bf16[4,128,128]{2,1,0:T(8,128)(2,1)S(1)} collective-permute-done((bf16[4,128,128]{2,1,0:T(8,128)(2,1)S(1)}, bf16[4,128,128]{2,1,0:T(8,128)(2,1)S(1)}, u32[]{:S(2)}, u32[]{:S(2)}) %collective-permute-start.8) | collective-permute-done | bytes 131104 | tf_op jit(solution)/shard_map/ppermute | solution.py:37
  28.4 1.9 %collective-permute-done.9.refs_10_ = bf16[4,128,128]{2,1,0:T(8,128)(2,1)S(1)} collective-permute-done((bf16[4,128,128]{2,1,0:T(8,128)(2,1)S(1)}, bf16[4,128,128]{2,1,0:T(8,128)(2,1)S(1)}, u32[]{:S(2)}, u32[]{:S(2)}) %collective-permute-start.9) | collective-permute-done | bytes 131104 | tf_op jit(solution)/shard_map/ppermute | solution.py:37
  30.4 0.5 collective-permute-start.15
  30.9 0.0 collective-permute-start.7
  30.9 0.5 collective-permute-start.12
  31.4 0.0 collective-permute-done.6.refs_5_
  31.4 0.0 collective-permute-start.13
  31.4 0.8 %collective-permute-done.7.refs_7_ = bf16[4,128,128]{2,1,0:T(8,128)(2,1)S(1)} collective-permute-done((bf16[4,128,128]{2,1,0:T(8,128)(2,1)S(1)}, bf16[4,128,128]{2,1,0:T(8,128)(2,1)S(1)}, u32[]{:S(2)}, u32[]{:S(2)}) %collective-permute-start.7) | collective-permute-done | bytes 131104 | tf_op jit(solution)/shard_map/ppermute | solution.py:37
  32.3 0.2 collective-permute-done.12.refs_9_
  32.4 0.3 collective-permute-done.13.refs_11_
  32.8 6.5 %shard_map.63 = (bf16[2,768,256]{2,1,0:T(8,128)(2,1)S(1)}, bf16[2,384,256]{2,1,0:T(8,128)(2,1)S(1)}, bf16[2,768,256]{2,1,0:T(8,128)(2,1)S(1)}, bf16[2,384,256]{2,1,0:T(8,128)(2,1)S(1)}, f32[9,384,256]{2,1,0:T(8,128)S(1)}) custom-call(s32[8]{0:T(128)S(1)} %stack.32.ids, bf16[4,128,128]{2,1,0:T(8,128)(2,1)S(1)} %get-tuple-element.55.refs_2_.refs_0_, ...), custom_call_target="tpu_custom_call" | custom-call | flops 1000 | bytes 1000 | tf_op jit(solution)/shard_map/pallas_call | solution.py:396
  39.3 0.1 collective-permute-done.14.refs_0_
  39.4 0.0 collective-permute-done.15.refs_14_
  39.4 1.5 %collective-permute-start.16 = (bf16[4,128,128]{2,1,0:T(8,128)(2,1)S(1)}, bf16[4,128,128]{2,1,0:T(8,128)(2,1)S(1)}, u32[]{:S(2)}, u32[]{:S(2)}) collective-permute-start(bf16[4,128,128]{2,1,0:T(8,128)(2,1)S(1)} %get-tuple-element.75.refs_0_), channel_id=1, source_target_pairs={{0,2},{2,0},{1,3},{3,1},{4,6},{6,4},{5,7},{7,5},{8,10},{10,8},{9,1... | collective-permute-start | bytes 393224 | tf_op jit(solution)/shard_map/ppermute | solution.py:37
  40.9 3.0 %shard_map.64 = bf16[128,4,128]{2,1,0:T(4,128)(2,1)} custom-call(s32[8]{0:T(128)S(1)} %stack.32.ids, bf16[4,128,128]{2,1,0:T(8,128)(2,1)S(1)} %get-tuple-element.45.refs_0_, bf16[4,128,128]{2,1,0:T(8,128)(2,1)S(1)} %collective-permute-done.refs_1_, bf16[4,128,128]{2,1,0:T(8,128)(2,1)S(1)} %collective-permute-done.1.refs_2_, ...), custom_call_target="tpu_custom_call" | custom-call | flops 1000 | bytes 1000 | tf_op jit(solution)/shard_map/pallas_call | solution.py:204
  43.8 1.1 %collective-permute-done.16.refs_4_ = bf16[4,128,128]{2,1,0:T(8,128)(2,1)S(1)} collective-permute-done((bf16[4,128,128]{2,1,0:T(8,128)(2,1)S(1)}, bf16[4,128,128]{2,1,0:T(8,128)(2,1)S(1)}, u32[]{:S(2)}, u32[]{:S(2)}) %collective-permute-start.16) | collective-permute-done | bytes 131104 | tf_op jit(solution)/shard_map/ppermute | solution.py:37
  45.0 0.0 collective-permute-start.17
  45.0 0.5 collective-permute-start.18
  45.5 0.0 collective-permute-start.19
  45.5 0.8 %collective-permute-done.17.refs_1_ = bf16[4,128,128]{2,1,0:T(8,128)(2,1)S(1)} collective-permute-done((bf16[4,128,128]{2,1,0:T(8,128)(2,1)S(1)}, bf16[4,128,128]{2,1,0:T(8,128)(2,1)S(1)}, u32[]{:S(2)}, u32[]{:S(2)}) %collective-permute-start.17) | collective-permute-done | bytes 131104 | tf_op jit(solution)/shard_map/ppermute | solution.py:37
  46.3 0.2 collective-permute-done.18.refs_3_
  46.5 0.3 collective-permute-done.19.refs_5_
  46.8 7.3 %shard_map.66 = (f32[128,6912]{1,0:T(8,128)}, bf16[128,4,128]{2,1,0:T(4,128)(2,1)}) custom-call(s32[8]{0:T(128)S(1)} %stack.32.ids, bf16[4,128,128]{2,1,0:T(8,128)(2,1)S(1)} %get-tuple-element.75.refs_0_, bf16[4,128,128]{2,1,0:T(8,128)(2,1)S(1)} %collective-permute-done.17.refs_1_, bf16[4,128,128]{2,1,0:T(8,128)(2,1)S(1)} %get-tuple-element.76.refs_2_, ...), custom_call_target="tpu_custom_call" | custom-call | flops 1000 | bytes 1000 | tf_op jit(solution)/shard_map/pallas_call | solution.py:396
  (2 shorter events, 0.1 us)
Async XLA Ops:
  0.6 0.9 %copy-start.1 = (bf16[128,4,128]{2,1,0:T(4,128)(2,1)S(1)}, bf16[128,4,128]{2,1,0:T(4,128)(2,1)}, u32[]{:S(2)}) copy-start(bf16[128,4,128]{2,1,0:T(4,128)(2,1)} %act_ref.1) | copy-start | bytes 393220
  1.5 0.9 %copy-start.2 = (bf16[128,4,128]{2,1,0:T(4,128)(2,1)S(1)}, bf16[128,4,128]{2,1,0:T(4,128)(2,1)}, u32[]{:S(2)}) copy-start(bf16[128,4,128]{2,1,0:T(4,128)(2,1)} %grad_ref.1) | copy-start | bytes 393220
  3.1 7.1 %collective-permute-start.1 = (bf16[4,128,128]{2,1,0:T(8,128)(2,1)S(1)}, bf16[4,128,128]{2,1,0:T(8,128)(2,1)S(1)}, u32[]{:S(2)}, u32[]{:S(2)}) collective-permute-start(bf16[4,128,128]{2,1,0:T(8,128)(2,1)S(1)} %get-tuple-element.45.refs_0_), channel_id=1, source_target_pairs={{0,2},{2,0},{1,3},{3,1},{4,6},{6,4},{5,7},{7,5},{8,10},{10,8},{9,1... | collective-permute-start | bytes 393224 | tf_op jit(solution)/shard_map/ppermute | solution.py:37
  6.1 11.1 %collective-permute-start.4 = (bf16[8,128,128]{2,1,0:T(8,128)(2,1)S(1)}, bf16[8,128,128]{2,1,0:T(8,128)(2,1)S(1)}, u32[]{:S(2)}, u32[]{:S(2)}) collective-permute-start(bf16[8,128,128]{2,1,0:T(8,128)(2,1)S(1)} %get-tuple-element.62), channel_id=1, source_target_pairs={{0,12},{4,8},{8,4},{12,0},{1,13},{5,9},{9,5},{13,1},{2,14},{6,10},... | collective-permute-start | bytes 786440 | tf_op jit(solution)/shard_map/ppermute | solution.py:30
  9.7 11.7 %collective-permute-start.3 = (bf16[8,128,128]{2,1,0:T(8,128)(2,1)S(1)}, bf16[8,128,128]{2,1,0:T(8,128)(2,1)S(1)}, u32[]{:S(2)}, u32[]{:S(2)}) collective-permute-start(bf16[8,128,128]{2,1,0:T(8,128)(2,1)S(1)} %get-tuple-element.62), channel_id=1, source_target_pairs={{0,4},{4,0},{8,12},{12,8},{1,5},{5,1},{9,13},{13,9},{2,6},{6,2},{1... | collective-permute-start | bytes 786440 | tf_op jit(solution)/shard_map/ppermute | solution.py:30
  9.7 4.1 %collective-permute-start = (bf16[4,128,128]{2,1,0:T(8,128)(2,1)S(1)}, bf16[4,128,128]{2,1,0:T(8,128)(2,1)S(1)}, u32[]{:S(2)}, u32[]{:S(2)}) collective-permute-start(bf16[4,128,128]{2,1,0:T(8,128)(2,1)S(1)} %get-tuple-element.45.refs_0_), channel_id=1, source_target_pairs={{0,1},{1,0},{2,3},{3,2},{4,5},{5,4},{6,7},{7,6},{8,9},{9,8},{10,11... | collective-permute-start | bytes 393224 | tf_op jit(solution)/shard_map/ppermute | solution.py:37
  9.7 4.1 %collective-permute-start.5 = (bf16[4,128,128]{2,1,0:T(8,128)(2,1)S(1)}, bf16[4,128,128]{2,1,0:T(8,128)(2,1)S(1)}, u32[]{:S(2)}, u32[]{:S(2)}) collective-permute-start(bf16[4,128,128]{2,1,0:T(8,128)(2,1)S(1)} %get-tuple-element.49.refs_4_.refs_0_), channel_id=1, source_target_pairs={{0,1},{1,0},{2,3},{3,2},{4,5},{5,4},{6,7},{7,6},{8,9},{9,8},{10,11... | collective-permute-start | bytes 393224 | tf_op jit(solution)/shard_map/ppermute | solution.py:37
  10.2 3.6 %collective-permute-start.2 = (bf16[4,128,128]{2,1,0:T(8,128)(2,1)S(1)}, bf16[4,128,128]{2,1,0:T(8,128)(2,1)S(1)}, u32[]{:S(2)}, u32[]{:S(2)}) collective-permute-start(bf16[4,128,128]{2,1,0:T(8,128)(2,1)S(1)} %collective-permute-done.1.refs_2_), channel_id=1, source_target_pairs={{0,1},{1,0},{2,3},{3,2},{4,5},{5,4},{6,7},{7,6},{8,9},{9,8},{10,11... | collective-permute-start | bytes 393224 | tf_op jit(solution)/shard_map/ppermute | solution.py:37
  10.3 1.5 %copy-start = (bf16[128,6912]{1,0:T(8,128)(2,1)S(1)}, bf16[128,6912]{1,0:T(8,128)(2,1)}, u32[]{:S(2)}) copy-start(bf16[128,6912]{1,0:T(8,128)(2,1)} %w_ref.1) | copy-start | bytes 5308420
  21.5 2.6 %collective-permute-start.10 = (bf16[4,128,128]{2,1,0:T(8,128)(2,1)S(1)}, bf16[4,128,128]{2,1,0:T(8,128)(2,1)S(1)}, u32[]{:S(2)}, u32[]{:S(2)}) collective-permute-start(bf16[4,128,128]{2,1,0:T(8,128)(2,1)S(1)} %get-tuple-element.55.refs_2_.refs_0_), channel_id=1, source_target_pairs={{0,1},{1,0},{2,3},{3,2},{4,5},{5,4},{6,7},{7,6},{8,9},{9,8},{10,11... | collective-permute-start | bytes 393224 | tf_op jit(solution)/shard_map/ppermute | solution.py:37
  21.6 3.2 %collective-permute-start.11 = (bf16[4,128,128]{2,1,0:T(8,128)(2,1)S(1)}, bf16[4,128,128]{2,1,0:T(8,128)(2,1)S(1)}, u32[]{:S(2)}, u32[]{:S(2)}) collective-permute-start(bf16[4,128,128]{2,1,0:T(8,128)(2,1)S(1)} %get-tuple-element.56.refs_4_.refs_2_), channel_id=1, source_target_pairs={{0,1},{1,0},{2,3},{3,2},{4,5},{5,4},{6,7},{7,6},{8,9},{9,8},{10,11... | collective-permute-start | bytes 393224 | tf_op jit(solution)/shard_map/ppermute | solution.py:37
  22.1 6.4 %collective-permute-start.8 = (bf16[4,128,128]{2,1,0:T(8,128)(2,1)S(1)}, bf16[4,128,128]{2,1,0:T(8,128)(2,1)S(1)}, u32[]{:S(2)}, u32[]{:S(2)}) collective-permute-start(bf16[4,128,128]{2,1,0:T(8,128)(2,1)S(1)} %get-tuple-element.53.refs_4_), channel_id=1, source_target_pairs={{0,2},{2,0},{1,3},{3,1},{4,6},{6,4},{5,7},{7,5},{8,10},{10,8},{9,1... | collective-permute-start | bytes 393224 | tf_op jit(solution)/shard_map/ppermute | solution.py:37
  22.6 7.8 %collective-permute-start.9 = (bf16[4,128,128]{2,1,0:T(8,128)(2,1)S(1)}, bf16[4,128,128]{2,1,0:T(8,128)(2,1)S(1)}, u32[]{:S(2)}, u32[]{:S(2)}) collective-permute-start(bf16[4,128,128]{2,1,0:T(8,128)(2,1)S(1)} %get-tuple-element.54.refs_6_), channel_id=1, source_target_pairs={{0,2},{2,0},{1,3},{3,1},{4,6},{6,4},{5,7},{7,5},{8,10},{10,8},{9,1... | collective-permute-start | bytes 393224 | tf_op jit(solution)/shard_map/ppermute | solution.py:37
  24.1 7.3 %collective-permute-start.6 = (bf16[4,128,128]{2,1,0:T(8,128)(2,1)S(1)}, bf16[4,128,128]{2,1,0:T(8,128)(2,1)S(1)}, u32[]{:S(2)}, u32[]{:S(2)}) collective-permute-start(bf16[4,128,128]{2,1,0:T(8,128)(2,1)S(1)} %get-tuple-element.53.refs_4_), channel_id=1, source_target_pairs={{0,1},{1,0},{2,3},{3,2},{4,5},{5,4},{6,7},{7,6},{8,9},{9,8},{10,11... | collective-permute-start | bytes 393224 | tf_op jit(solution)/shard_map/ppermute | solution.py:37
  24.1 15.2 %collective-permute-start.14 = (bf16[8,128,128]{2,1,0:T(8,128)(2,1)S(1)}, bf16[8,128,128]{2,1,0:T(8,128)(2,1)S(1)}, u32[]{:S(2)}, u32[]{:S(2)}) collective-permute-start(bf16[8,128,128]{2,1,0:T(8,128)(2,1)S(1)} %get-tuple-element.62), channel_id=1, source_target_pairs={{0,8},{4,12},{8,0},{12,4},{1,9},{5,13},{9,1},{13,5},{2,10},{6,14},... | collective-permute-start | bytes 786440 | tf_op jit(solution)/shard_map/ppermute | solution.py:30
  30.4 9.0 %collective-permute-start.15 = (f32[128,512]{1,0:T(8,128)S(1)}, f32[128,512]{1,0:T(8,128)S(1)}, u32[]{:S(2)}, u32[]{:S(2)}) collective-permute-start(f32[128,512]{1,0:T(8,128)S(1)} %get-tuple-element.69), channel_id=1, source_target_pairs={{0,2},{2,0},{1,3},{3,1},{4,6},{6,4},{5,7},{7,5},{8,10},{10,8},{9,1... | collective-permute-start | bytes 786440 | tf_op jit(solution)/shard_map/ppermute | solution.py:37
  30.9 1.3 %collective-permute-start.7 = (bf16[4,128,128]{2,1,0:T(8,128)(2,1)S(1)}, bf16[4,128,128]{2,1,0:T(8,128)(2,1)S(1)}, u32[]{:S(2)}, u32[]{:S(2)}) collective-permute-start(bf16[4,128,128]{2,1,0:T(8,128)(2,1)S(1)} %get-tuple-element.54.refs_6_), channel_id=1, source_target_pairs={{0,1},{1,0},{2,3},{3,2},{4,5},{5,4},{6,7},{7,6},{8,9},{9,8},{10,11... | collective-permute-start | bytes 393224 | tf_op jit(solution)/shard_map/ppermute | solution.py:37
  30.9 1.5 %collective-permute-start.12 = (bf16[4,128,128]{2,1,0:T(8,128)(2,1)S(1)}, bf16[4,128,128]{2,1,0:T(8,128)(2,1)S(1)}, u32[]{:S(2)}, u32[]{:S(2)}) collective-permute-start(bf16[4,128,128]{2,1,0:T(8,128)(2,1)S(1)} %collective-permute-done.8.refs_8_), channel_id=1, source_target_pairs={{0,1},{1,0},{2,3},{3,2},{4,5},{5,4},{6,7},{7,6},{8,9},{9,8},{10,11... | collective-permute-start | bytes 393224 | tf_op jit(solution)/shard_map/ppermute | solution.py:37
  31.4 1.3 %collective-permute-start.13 = (bf16[4,128,128]{2,1,0:T(8,128)(2,1)S(1)}, bf16[4,128,128]{2,1,0:T(8,128)(2,1)S(1)}, u32[]{:S(2)}, u32[]{:S(2)}) collective-permute-start(bf16[4,128,128]{2,1,0:T(8,128)(2,1)S(1)} %collective-permute-done.9.refs_10_), channel_id=1, source_target_pairs={{0,1},{1,0},{2,3},{3,2},{4,5},{5,4},{6,7},{7,6},{8,9},{9,8},{10,11... | collective-permute-start | bytes 393224 | tf_op jit(solution)/shard_map/ppermute | solution.py:37
  39.4 5.6 %collective-permute-start.16 = (bf16[4,128,128]{2,1,0:T(8,128)(2,1)S(1)}, bf16[4,128,128]{2,1,0:T(8,128)(2,1)S(1)}, u32[]{:S(2)}, u32[]{:S(2)}) collective-permute-start(bf16[4,128,128]{2,1,0:T(8,128)(2,1)S(1)} %get-tuple-element.75.refs_0_), channel_id=1, source_target_pairs={{0,2},{2,0},{1,3},{3,1},{4,6},{6,4},{5,7},{7,5},{8,10},{10,8},{9,1... | collective-permute-start | bytes 393224 | tf_op jit(solution)/shard_map/ppermute | solution.py:37
  45.0 1.3 %collective-permute-start.17 = (bf16[4,128,128]{2,1,0:T(8,128)(2,1)S(1)}, bf16[4,128,128]{2,1,0:T(8,128)(2,1)S(1)}, u32[]{:S(2)}, u32[]{:S(2)}) collective-permute-start(bf16[4,128,128]{2,1,0:T(8,128)(2,1)S(1)} %get-tuple-element.75.refs_0_), channel_id=1, source_target_pairs={{0,1},{1,0},{2,3},{3,2},{4,5},{5,4},{6,7},{7,6},{8,9},{9,8},{10,11... | collective-permute-start | bytes 393224 | tf_op jit(solution)/shard_map/ppermute | solution.py:37
  45.0 1.5 %collective-permute-start.18 = (bf16[4,128,128]{2,1,0:T(8,128)(2,1)S(1)}, bf16[4,128,128]{2,1,0:T(8,128)(2,1)S(1)}, u32[]{:S(2)}, u32[]{:S(2)}) collective-permute-start(bf16[4,128,128]{2,1,0:T(8,128)(2,1)S(1)} %get-tuple-element.76.refs_2_), channel_id=1, source_target_pairs={{0,1},{1,0},{2,3},{3,2},{4,5},{5,4},{6,7},{7,6},{8,9},{9,8},{10,11... | collective-permute-start | bytes 393224 | tf_op jit(solution)/shard_map/ppermute | solution.py:37
  45.5 1.3 %collective-permute-start.19 = (bf16[4,128,128]{2,1,0:T(8,128)(2,1)S(1)}, bf16[4,128,128]{2,1,0:T(8,128)(2,1)S(1)}, u32[]{:S(2)}, u32[]{:S(2)}) collective-permute-start(bf16[4,128,128]{2,1,0:T(8,128)(2,1)S(1)} %collective-permute-done.16.refs_4_), channel_id=1, source_target_pairs={{0,1},{1,0},{2,3},{3,2},{4,5},{5,4},{6,7},{7,6},{8,9},{9,8},{10,11... | collective-permute-start | bytes 393224 | tf_op jit(solution)/shard_map/ppermute | solution.py:37
